TPU v7x, 512 devices: a whole 4x4x16 slice. The times are simulated.
512 devices in a mesh: dp: 8 (over z_lo, core), axial: 64 (over x, y, z_hi).
Axes of the slice: x: 4, y: 4, z: 16 (z_hi: 4, z_lo: 4; z = z_hi * 4 + z_lo), core: 2. Of those that a mesh axis runs over, the one named last changes fastest.
Arguments:
- pair: float32 [1024, 128, 128], P(('dp', 'axial')), parts along dimension 0, may hold values from -36 to 36
- cotangent: float32 [1024, 128, 128], P(('dp', 'axial')), parts along dimension 0, may hold values from -16 to 16
- norm_gain: float32 [2, 128], replicated, may hold values from 0.5 to 1.5
- norm_shift: float32 [2, 128], replicated, may hold values from -3 to 3
- weight_in: float32 [2, 128, 512], replicated, may hold values from -0.5 to 0.5
- weight_bias: float32 [2, 128, 4], replicated, may hold values from -0.5 to 0.5
- gate_shift: float32 [2, 128], replicated, may hold values from -4 to 4
- weight_out: float32 [2, 128, 128], replicated, may hold values from -0.5 to 0.5
Outputs:
- final: float32 [1024, 128, 128], P(('dp', 'axial')), parts along dimension 0
- grad_pair: float32 [1024, 128, 128], P(('dp', 'axial')), parts along dimension 0
- grad_in: float32 [16, 128, 512], P('dp'), parts along dimension 0
- grad_bias: float32 [16, 128, 4], P('dp'), parts along dimension 0
- grad_out: float32 [16, 128, 128], P('dp'), parts along dimension 0
There are 8 independent parts, one for each index of `dp`. A program takes and returns all parts, laid end to end along the dimension named above; an argument that names none is the same for every part. Nothing has to cross between parts.
All inputs are finite; a program needn't handle non-finite values.
Results may differ from a plain program's by a relative error of at most 0.00014.
Values sent between devices are 32-bit elements; how exact they have to be, the bound alone decides.
No kernel may reach another device: no remote copies, remote signals or barrier semaphores. Data moves between devices by JAX's collectives and lax.ppermute only.
A program may use at most 64 MiB of HBM per device.

v0:
```python
import jax
import jax.numpy as jnp
from jax import lax
from jax.sharding import PartitionSpec as P

highest = lax.Precision.HIGHEST


def normed(pair_in, norm_gain, norm_shift):
    centre = pair_in - jnp.mean(pair_in, axis=-1, keepdims=True)
    spread = jnp.mean(centre * centre, axis=-1, keepdims=True)
    return centre * lax.rsqrt(spread + 1e-05) * norm_gain + norm_shift


def pair_bias(pair_in, norm_gain, norm_shift, weight_bias):
    return jnp.einsum(
        "rjc,ch->rjh", normed(pair_in, norm_gain, norm_shift), weight_bias, precision=highest
    )


def attend(pair_in, norm_gain, norm_shift, weight_in, gate_shift, weight_out, bias_full):
    row_count, col_count, channels = pair_in.shape
    head_count = bias_full.shape[-1]
    head_size = channels // head_count
    normal_in = normed(pair_in, norm_gain, norm_shift)
    projected = jnp.einsum("rjc,ce->rje", normal_in, weight_in, precision=highest)
    queries, keys_all, values_all, gate_raw = jnp.split(projected, 4, axis=-1)
    split_shape = (row_count, col_count, head_count, head_size)
    queries = queries.reshape(split_shape)
    keys_all = keys_all.reshape(split_shape)
    values_all = values_all.reshape(split_shape)
    logits = jnp.einsum("rjhd,rkhd->rhjk", queries, keys_all, precision=highest) * head_size ** (
        -0.5
    )
    logits = logits + jnp.transpose(bias_full, (2, 0, 1))[None]
    exponent = jnp.exp(logits)
    attention = exponent / jnp.sum(exponent, axis=-1, keepdims=True)
    mixture = jnp.einsum("rhjk,rkhd->rjhd", attention, values_all, precision=highest).reshape(
        row_count, col_count, channels
    )
    gated_out = jax.nn.sigmoid(gate_raw + gate_shift) * mixture
    return pair_in + jnp.einsum("rjc,cd->rjd", gated_out, weight_out, precision=highest)


def attend_rows(pair_in, norm_gain, norm_shift, weight_in, gate_shift, weight_out, bias_full):

    def one_row(row_in):
        return attend(
            row_in[None], norm_gain, norm_shift, weight_in, gate_shift, weight_out, bias_full
        )[0]

    return lax.map(jax.checkpoint(one_row), pair_in)


def flip_layout(block):
    turned = jnp.transpose(block, (1, 0, 2))
    return lax.all_to_all(turned, "axial", split_axis=0, concat_axis=1, tiled=True)


def regather(pair_in, norm_gain, norm_shift, weight_bias):
    return lax.all_gather(
        pair_bias(pair_in, norm_gain, norm_shift, weight_bias), "axial", axis=0, tiled=True
    )


def module_back(
    pair_in,
    norm_gain,
    norm_shift,
    weight_in,
    weight_bias,
    gate_shift,
    weight_out,
    bias_full,
    upstream,
):
    unused_out, attend_back = jax.vjp(
        attend_rows, pair_in, norm_gain, norm_shift, weight_in, gate_shift, weight_out, bias_full
    )
    grads_attend = attend_back(upstream)
    grad_local = lax.psum_scatter(grads_attend[6], "axial", scatter_dimension=0, tiled=True)
    unused_bias, bias_back = jax.vjp(pair_bias, pair_in, norm_gain, norm_shift, weight_bias)
    grads_bias = bias_back(grad_local)
    return (grads_attend[0] + grads_bias[0], grads_attend[3], grads_bias[3], grads_attend[5])


def body(pair, cotangent, norm_gain, norm_shift, weight_in, weight_bias, gate_shift, weight_out):
    local_first = pair_bias(pair, norm_gain[0], norm_shift[0], weight_bias[0])
    bias_first = lax.all_gather(local_first, "axial", axis=0, tiled=True)
    first_out = attend_rows(
        pair, norm_gain[0], norm_shift[0], weight_in[0], gate_shift[0], weight_out[0], bias_first
    )
    flipped = flip_layout(first_out)
    local_second = pair_bias(flipped, norm_gain[1], norm_shift[1], weight_bias[1])
    bias_second = lax.all_gather(local_second, "axial", axis=0, tiled=True)
    second_out = attend_rows(
        flipped,
        norm_gain[1],
        norm_shift[1],
        weight_in[1],
        gate_shift[1],
        weight_out[1],
        bias_second,
    )
    final = flip_layout(second_out)
    cot_flipped = flip_layout(cotangent)
    saved_second = regather(flipped, norm_gain[1], norm_shift[1], weight_bias[1])
    saved_first = regather(pair, norm_gain[0], norm_shift[0], weight_bias[0])
    grads_second = module_back(
        flipped,
        norm_gain[1],
        norm_shift[1],
        weight_in[1],
        weight_bias[1],
        gate_shift[1],
        weight_out[1],
        saved_second,
        cot_flipped,
    )
    grad_first_out = flip_layout(grads_second[0])
    grads_first = module_back(
        pair,
        norm_gain[0],
        norm_shift[0],
        weight_in[0],
        weight_bias[0],
        gate_shift[0],
        weight_out[0],
        saved_first,
        grad_first_out,
    )
    stacked_in = jnp.stack([grads_first[1], grads_second[1]])
    stacked_bias = jnp.stack([grads_first[2], grads_second[2]])
    stacked_out = jnp.stack([grads_first[3], grads_second[3]])
    summed = lax.psum((stacked_in, stacked_bias, stacked_out), "axial")
    factor = 1.0 / pair.shape[1]
    return (final, grads_first[0], summed[0] * factor, summed[1] * factor, summed[2] * factor)


def solution(mesh):
    in_specs = (
        P(("dp", "axial"), None, None),
        P(("dp", "axial"), None, None),
        P(),
        P(),
        P(),
        P(),
        P(),
        P(),
    )
    out_specs = (
        P(("dp", "axial"), None, None),
        P(("dp", "axial"), None, None),
        P("dp", None, None),
        P("dp", None, None),
        P("dp", None, None),
    )
    return jax.shard_map(body, mesh=mesh, in_specs=in_specs, out_specs=out_specs, check_vma=False)
```

profile of v0, /device:TPU:64, one launch (start us, length us, event | category | flops | bytes accessed | tf_op | source)
XLA Modules:
  0.0 2450.4 jit_solution(11486570986585576043)
XLA Ops:
  11.1 227.4 %all_gather.8 = f32[128,128,4]{1,2,0:T(4,128)S(1)} all-gather(f32[2,128,4]{1,2,0:T(4,128)S(1)} %fusion.124), channel_id=1, replica_groups=mesh['dp'=8,'axial'=64] {'axial'}, dimensions={0}, use_global_device_ids=true | all-gather | bytes 266240 | tf_op jit(solution)/shard_map/all_gather | solution.py:89
  241.4 10.4 while.62
  243.7 2.8 dynamic_update_slice.33
  248.9 2.8 dynamic_update_slice.33
  252.4 4.6 all-to-all-start
  257.8 18.0 all-to-all-done
  275.8 4.6 all-to-all-start.2
  282.3 223.9 %all_gather.9 = f32[128,128,4]{1,2,0:T(4,128)S(1)} all-gather(f32[2,128,4]{1,2,0:T(4,128)S(1)} %fusion.146), channel_id=1, replica_groups=mesh['dp'=8,'axial'=64] {'axial'}, dimensions={0}, use_global_device_ids=true | all-gather | bytes 266240 | tf_op jit(solution)/shard_map/all_gather | solution.py:95
  507.8 25.4 %while.64 = (s32[]{:T(128)}, f32[128,512]{1,0:T(8,128)S(1)}, f32[128,128,4]{0,1,2:T(8,128)S(1)}, f32[128,128]{1,0:T(8,128)}, f32[2,128,128]{1,2,0:T(8,128)}, /*i...) while((s32[]{:T(128)}, f32[128,512]{1,0:T(8,128)S(1)}, ...), condition=%wide.region_21.22_spmd.clone, body=%wide.region_14.21_spmd.clone.sunk | while | flops 506021248 | bytes 12461153 | solution.py:52
  536.4 780.5 %all-reduce.6.cloned.1.call-done = f32[128,128,4]{1,2,0:T(4,128)} async-done(((f32[128,128,4]{1,2,0:T(4,128)}), f32[128,128,4]{1,2,0:T(4,128)}) %all-reduce.6.cloned.1.call-update) | async-done | bytes 262160
  1319.6 8.5 all-to-all-start.3
  1328.5 17.5 all-to-all-done.3
  1347.6 38.4 %while.65 = (s32[]{:T(128)}, f32[128,512]{1,0:T(8,128)S(1)}, f32[128,128,4]{0,1,2:T(8,128)S(1)}, f32[128,128]{1,0:T(8,128)}, f32[2,128,128]{1,2,0:T(8,128)}, /*i...) while((s32[]{:T(128)}, f32[128,512]{1,0:T(8,128)S(1)}, ...), condition=%wide.region_32.33_spmd.clone, body=%wide.region_25.32_spmd.clone.sunk | while | flops 506021248 | bytes 12977217 | solution.py:52
  1352.8 1.4 multiply_reduce_fusion.26
  1356.3 1.9 fusion.349
  1375.5 1.9 fusion.349
  1389.2 10.4 while.63
  1391.6 2.8 dynamic_update_slice.34
  1396.8 2.8 dynamic_update_slice.34
  1399.7 4.8 all-to-all-start.1
  1405.4 16.7 all-to-all-done.1
  1422.9 793.6 %all-reduce.8.cloned.1.call-done = (f32[128,128,4]{1,2,0:T(4,128)}, f32[2,128,512]{2,1,0:T(8,128)}, f32[2,128,128]{2,1,0:T(8,128)}) async-done(((f32[128,128,4]{1,2,0:T(4,128)}, f32[2,128,512]{2,1,0:T(8,128)}, f32[2,128,128]{2,1,0:T(8,128)}), (f32[128,128,4]{1,2,0:T(4,128)}, f32[2,128,512]{2,1,0:T(8,128)}, f32[2,128,128]{2,1,0:T(8,128)})) %all-reduce.8.cloned.1.call-update) | async-done | bytes 917520
  2218.5 219.4 %psum.22 = f32[2,128,4]{1,2,0:T(4,128)S(1)} all-reduce(f32[2,128,4]{1,2,0:T(4,128)S(1)} %pad_maximum_fusion.2), channel_id=1, replica_groups=mesh['dp'=8,'axial'=64] {'axial'}, use_global_device_ids=true, to_apply=%region_37.38 | all-reduce | flops 1024 | bytes 8192 | tf_op jit(solution)/shard_map/psum | solution.py:135
  2438.5 1.9 broadcast_multiply_fusion.4
  (453 shorter events, 95.8 us)
Async XLA Ops:
  8.4 231.3 %copy-start.15 = (f32[2,128,512]{2,1,0:T(8,128)S(1)}, f32[2,128,512]{2,1,0:T(8,128)}, u32[]{:S(2)}) copy-start(f32[2,128,512]{2,1,0:T(8,128)} %param.20) | copy-start | bytes 1572868
  251.7 5.3 copy-start.31
  252.4 23.4 all-to-all-start
  275.8 230.7 %all-to-all-start.2 = ((f32[128,2,128]{2,1,0:T(2,128)}), f32[128,2,128]{2,1,0:T(2,128)S(1)}, u32[]{:S(2)}, u32[]{:S(2)}) async-start(f32[128,2,128]{2,1,0:T(2,128)} %bitcast.313), calls=%async_computation.2 | async-start | bytes 262144 | tf_op jit(solution)/shard_map/all_to_all | solution.py:57
  280.4 1036.5 %all-reduce.6.cloned.1.call-start = ((), (), s32[]{:S(2)}) async-start(), calls=%async_computation.4 | async-start | bytes 524288
  507.8 3.5 copy-start.6
  507.8 3.5 copy-start.49
  520.5 3.5 copy-start.6
  520.5 3.5 copy-start.49
  533.2 783.6 %copy-start.25 = (f32[128]{0:T(128)}, f32[128]{0:T(128)S(1)}, u32[]{:S(2)}) copy-start(f32[128]{0:T(128)S(1)} %get-tuple-element.1615) | copy-start | bytes 1540
  533.2 784.8 %copy-start.4 = (f32[2,128,128]{1,2,0:T(8,128)}, f32[2,128,128]{1,2,0:T(8,128)S(1)}, u32[]{:S(2)}) copy-start(f32[2,128,128]{1,2,0:T(8,128)S(1)} %get-tuple-element.1583) | copy-start | bytes 393220
  534.1 2.1 copy-start.22
  536.2 781.8 %copy-start.53 = (f32[2,128]{1,0:T(2,128)}, f32[2,128]{1,0:T(2,128)S(1)}, u32[]{:S(2)}) copy-start(f32[2,128]{1,0:T(2,128)S(1)} %div.262) | copy-start | bytes 3076
  536.3 780.6 %copy-start.60 = (f32[2,128,4]{1,2,0:T(4,128)S(1)}, f32[2,128,4]{1,2,0:T(4,128)}, u32[]{:S(2)}) copy-start(f32[2,128,4]{1,2,0:T(4,128)} %param.21) | copy-start | bytes 12292
  1319.6 26.3 %all-to-all-start.3 = ((f32[128,2,128]{2,1,0:T(2,128)}), f32[128,2,128]{2,1,0:T(2,128)S(1)}, u32[]{:S(2)}, u32[]{:S(2)}) async-start(f32[128,2,128]{2,1,0:T(2,128)} %copy.203), calls=%async_computation.3 | async-start | bytes 262144 | tf_op jit(solution)/shard_map/all_to_all | solution.py:57
  1328.2 888.3 %all-reduce.8.cloned.1.call-start = ((), (), s32[]{:S(2)}) async-start(), calls=%async_computation.5 | async-start | bytes 1835008
  1399.6 4.8 copy-start.5
  1399.6 4.8 copy-start.26
  1399.6 4.8 copy-start.36
  1399.6 4.8 copy-start.54
  1399.7 4.8 copy-start.65
  1399.7 22.5 all-to-all-start.1
  1422.1 794.3 %copy-start.63 = (f32[2,128]{1,0:T(2,128)S(1)}, f32[2,128]{1,0:T(2,128)}, u32[]{:S(2)}) copy-start(f32[2,128]{1,0:T(2,128)} %copy-done.62) | copy-start | bytes 3076
  1422.8 793.6 %copy-start.46 = (f32[2,128]{1,0:T(2,128)S(1)}, f32[2,128]{1,0:T(2,128)}, u32[]{:S(2)}) copy-start(f32[2,128]{1,0:T(2,128)} %copy-done.45) | copy-start | bytes 3076
  (82 other events, 70.7 us)
Sparse Core Ops, SparseCore 0:
  534.2 782.5 all-reduce.5
  1388.5 827.8 all-reduce.7
where the time goes:
time: 2450 us
  waiting for transfers between devices  1630 us (67%)
  blocking collectives  671 us (27%)
  local copies, waits for them, and re-layouts  60.4 us (2%)
  matrix products  44.5 us (2%)
    unnamed x4, waiting for transfers between devices  1570 us
    all_gather x1, blocking collectives, body(): bias_first = lax.all_gather(local_first, 'axial', axis=0, tiled=True)  227 us
    all_gather x1, blocking collectives, body(): bias_second = lax.all_gather(local_second, 'axial', axis=0, tiled=True)  224 us
    psum x1, blocking collectives, body(): summed = lax.psum((stacked_in, stacked_bias, stacked_out), 'axial')  219 us
    all_to_all x4, waiting for transfers between devices, flip_layout(): lax.all_to_all(turned, 'axial', split_axis=0, concat_axis=1, tiled=True)  52.2 us
  transfers between devices with their start and end apart: 6, of which 5 were waited for; matrix products, arithmetic and copies ran while one was open for 1% of the time, Pallas kernels for 0%

commit v1 on v0

v1 whole, which is shorter than its diff:
```python
import jax
import jax.numpy as jnp
from jax import lax
from jax.experimental import pallas as pl
from jax.experimental.pallas import tpu as pltpu
from jax.sharding import PartitionSpec as P

f32 = jnp.float32
both = ("dp", "axial")
homes = (
    (5, (2, 0, 1, 3)),
    (7, (2, 3, 0, 1)),
    (1, (0, 2, 3, 1)),
    (3, (0, 1, 2, 3)),
    (6, (2, 0, 1, 3)),
    (0, (2, 3, 0, 1)),
    (4, (0, 1, 2, 3)),
    (2, (0, 2, 3, 1)),
)


def compact_id(part, rank):
    block, places = homes[part]
    place = places[rank % 4]
    z = 2 * block + place // 2
    return ((z % 4) * 2 + place % 2) * 64 + (rank // 4) * 4 + z // 4


def plans(mesh):
    parts, size = mesh.shape["dp"], mesh.shape["axial"]
    if (parts, size) == (8, 64):
        placed = [[compact_id(c, r) for r in range(64)] for c in range(8)]
    else:
        placed = [[c * size + r for r in range(size)] for c in range(parts)]
    there = [(c * size + r, placed[c][r]) for c in range(parts) for r in range(size)]
    back = [(b, a) for a, b in there]
    fours = [ids[4 * b : 4 * b + 4] for ids in placed for b in range(16)]
    planes = [[c * size + 4 * b + k for b in range(16)] for c in range(parts) for k in range(4)]
    return placed, there, back, fours, planes


def dot(a, b, ca, cb):
    return lax.dot_general(
        a, b, (((ca,), (cb,)), ((), ())), precision=lax.Precision.HIGH, preferred_element_type=f32
    )


def norm_parts(x):
    centre = x - jnp.mean(x, axis=-1, keepdims=True)
    root = lax.rsqrt(jnp.mean(centre * centre, axis=-1, keepdims=True) + 1e-05)
    return centre * root, root


def norm_back(dy, gain, unit, root):
    du = dy * gain
    return root * (
        du
        - jnp.mean(du, axis=-1, keepdims=True)
        - unit * jnp.mean(du * unit, axis=-1, keepdims=True)
    )


def by_head(a):
    lane = lax.broadcasted_iota(jnp.int32, a.shape, 1) // 32
    return jnp.concatenate([jnp.where(lane == h, a, 0.0) for h in range(4)], axis=0)


def side_by_side(a):
    return jnp.concatenate([a[128 * h : 128 * h + 128] for h in range(4)], axis=1)


SCALE = 32**-0.5


def probabilities(q, k, bias, keys_down):
    if keys_down:
        e = jnp.exp(dot(by_head(k), q, 1, 1) * SCALE + bias)
        total = jnp.sum(e.reshape(4, 128, 128), axis=1, keepdims=True)
        return (e.reshape(4, 128, 128) * (1.0 / total)).reshape(512, 128)
    e = jnp.exp(dot(by_head(q), k, 1, 1) * SCALE + bias)
    return e * (1.0 / jnp.sum(e, axis=1, keepdims=True))


def mix(probs, v, keys_down):
    if keys_down:
        return dot(probs, by_head(v), 0, 0)
    return dot(side_by_side(probs), by_head(v), 1, 0)


def attention_back(do, q, k, v, probs, keys_down):
    if keys_down:
        dp = dot(by_head(v), do, 1, 1)
        both_p = (probs * dp).reshape(4, 128, 128)
        ds = (both_p - probs.reshape(4, 128, 128) * jnp.sum(both_p, axis=1, keepdims=True)).reshape(
            512, 128
        )
        dv = dot(side_by_side(probs), by_head(do), 1, 0)
        dk = dot(side_by_side(ds), by_head(q), 1, 0) * SCALE
        dq = dot(ds, by_head(k), 0, 0) * SCALE
    else:
        dp = dot(by_head(do), v, 1, 1)
        both_p = probs * dp
        ds = both_p - probs * jnp.sum(both_p, axis=1, keepdims=True)
        dv = dot(probs, by_head(do), 0, 0)
        dk = dot(ds, by_head(q), 0, 0) * SCALE
        dq = dot(side_by_side(ds), by_head(k), 1, 0) * SCALE
    return ds, dq, dk, dv


def gather_rows(ref, first, stride):
    a, b = first
    return jnp.concatenate([ref[pl.ds(a, 64, stride=stride), :], ref[pl.ds(b, 64, stride=stride), :]])


def scatter_rows(ref, first, stride, value):
    a, b = first
    ref[pl.ds(a, 64, stride=stride), :] = value[:64]
    ref[pl.ds(b, 64, stride=stride), :] = value[64:]


def start_kernel(xin, gain, shift, wbias, out):
    rows = []
    for r in range(2):
        x = gather_rows(xin, (r * 128, r * 128 + 1), 2)
        unit, root = norm_parts(x)
        rows.append(dot(wbias[0], unit * gain[0:1, :] + shift[0:1, :], 1, 1))
    block = jnp.concatenate(rows, axis=0)
    for q in range(64):
        out[q * 8 : q * 8 + 8, :] = block


def first_kernel(
    xin, brecv, gain, shift, win, wbias, gate, wout, send, proj_o, probs_o, mixed_o, first_o
):
    bias = jnp.concatenate([gather_rows(brecv, (h, 4 + h), 8) for h in range(4)])
    x = jnp.concatenate([gather_rows(xin, (r * 128, r * 128 + 1), 2) for r in range(2)])
    unit, root = norm_parts(x)
    proj = dot(unit * gain[0:1, :] + shift[0:1, :], win[0], 1, 0)
    proj_o[...] = proj
    mixed = []
    for r in range(2):
        part = proj[r * 128 : r * 128 + 128]
        probs = probabilities(part[:, 0:128], part[:, 128:256], bias, False)
        probs_o[r * 512 : r * 512 + 512, :] = probs
        mixed.append(mix(probs, part[:, 256:384], False))
    mixed = jnp.concatenate(mixed)
    mixed_o[...] = mixed
    gated = jax.nn.sigmoid(proj[:, 384:512] + gate[0:1, :]) * mixed
    first = x + dot(gated, wout[0], 1, 0)
    first_o[...] = first
    unit1, root1 = norm_parts(first)
    y1 = unit1 * gain[1:2, :] + shift[1:2, :]
    bias_rows = jnp.concatenate(
        [dot(wbias[1], y1[r * 128 : r * 128 + 128], 1, 1) for r in range(2)], axis=0
    )
    for q in range(64):
        send[q * 16 + 4 : q * 16 + 12, :] = bias_rows
    for r in range(2):
        scatter_rows(send, (r * 2, r * 2 + 1), 16, first[r * 128 : r * 128 + 128])
        cot = gather_rows(xin, (256 + r * 128, 256 + r * 128 + 1), 2)
        scatter_rows(send, (12 + r * 2, 12 + r * 2 + 1), 16, cot)


def second_kernel(recv, gain, shift, win, gate, wout, send, wgrad):
    bias = jnp.concatenate([gather_rows(recv, (4 + h, 8 + h), 16) for h in range(4)])
    x = jnp.concatenate([gather_rows(recv, (c, 2 + c), 16) for c in range(2)])
    up = jnp.concatenate([gather_rows(recv, (12 + c, 14 + c), 16) for c in range(2)])
    unit, root = norm_parts(x)
    y = unit * gain[1:2, :] + shift[1:2, :]
    proj = dot(y, win[1], 1, 0)
    probs, mixed = [], []
    for c in range(2):
        part = proj[c * 128 : c * 128 + 128]
        probs.append(probabilities(part[:, 0:128], part[:, 128:256], bias, True))
        mixed.append(mix(probs[c], part[:, 256:384], True))
    mixed = jnp.concatenate(mixed)
    sig = jax.nn.sigmoid(proj[:, 384:512] + gate[1:2, :])
    gated = sig * mixed
    final = x + dot(gated, wout[1], 1, 0)
    dgated = dot(up, wout[1], 1, 1)
    dout = dot(gated, up, 0, 0)
    dmixed = dgated * sig
    dgate = dgated * mixed * sig * (1.0 - sig)
    dproj, dbias = [], 0.0
    for c in range(2):
        part = proj[c * 128 : c * 128 + 128]
        ds, dq, dk, dv = attention_back(
            dmixed[c * 128 : c * 128 + 128],
            part[:, 0:128],
            part[:, 128:256],
            part[:, 256:384],
            probs[c],
            True,
        )
        dbias = dbias + ds
        dproj.append(jnp.concatenate([dq, dk, dv, dgate[c * 128 : c * 128 + 128]], axis=1))
    dproj = jnp.concatenate(dproj)
    din = dot(y, dproj, 0, 0)
    dx = up + norm_back(dot(dproj, win[1], 1, 1), gain[1:2, :], unit, root)
    for c in range(2):
        scatter_rows(send, (c, 2 + c), 16, dx[c * 128 : c * 128 + 128])
        scatter_rows(send, (12 + c, 14 + c), 16, final[c * 128 : c * 128 + 128])
    for h in range(4):
        scatter_rows(send, (4 + h, 8 + h), 16, dbias[h * 128 : h * 128 + 128])
    for e in range(4):
        wgrad[e * 128 : e * 128 + 128, :] = din[:, e * 128 : e * 128 + 128]
    wgrad[512:640, :] = dout


def third_kernel(
    recv, xin, first, proj_s, probs_s, mixed_s, wgrad, gain, shift, win, wbias, gate, wout, send, dx_o, final_o
):
    for r in range(2):
        for c in range(2):
            final_o[pl.ds(r * 128 + c, 64, stride=2), :] = recv[pl.ds(12 + 2 * r + c, 64, stride=16), :]
    summed = jnp.sum(recv[...].reshape(64, 16, 128)[:, 4:12, :], axis=0)
    unit1, root1 = norm_parts(first[...])
    y1 = unit1 * gain[1:2, :] + shift[1:2, :]
    dy1 = jnp.concatenate([dot(summed[4 * r : 4 * r + 4], wbias[1], 0, 0) for r in range(2)])
    gb1 = dot(summed[0:4], y1[:128], 1, 0) + dot(summed[4:8], y1[128:], 1, 0)
    up = jnp.concatenate([gather_rows(recv, (2 * r, 2 * r + 1), 16) for r in range(2)])
    up = up + norm_back(dy1, gain[1:2, :], unit1, root1)
    x = jnp.concatenate([gather_rows(xin, (r * 128, r * 128 + 1), 2) for r in range(2)])
    unit, root = norm_parts(x)
    y = unit * gain[0:1, :] + shift[0:1, :]
    proj = proj_s[...]
    mixed = mixed_s[...]
    sig = jax.nn.sigmoid(proj[:, 384:512] + gate[0:1, :])
    dgated = dot(up, wout[0], 1, 1)
    dout = dot(sig * mixed, up, 0, 0)
    dmixed = dgated * sig
    dgate = dgated * mixed * sig * (1.0 - sig)
    dproj, dbias = [], 0.0
    for r in range(2):
        part = proj[r * 128 : r * 128 + 128]
        ds, dq, dk, dv = attention_back(
            dmixed[r * 128 : r * 128 + 128],
            part[:, 0:128],
            part[:, 128:256],
            part[:, 256:384],
            probs_s[r * 512 : r * 512 + 512, :],
            False,
        )
        dbias = dbias + ds
        dproj.append(jnp.concatenate([dq, dk, dv, dgate[r * 128 : r * 128 + 128]], axis=1))
    dproj = jnp.concatenate(dproj)
    din = dot(y, dproj, 0, 0)
    dx_o[...] = up + norm_back(dot(dproj, win[0], 1, 1), gain[0:1, :], unit, root)
    for h in range(4):
        scatter_rows(send, (h, 4 + h), 32, dbias[h * 128 : h * 128 + 128])
    for i in range(10):
        source = din[64 * (i % 2) : 64 * (i % 2) + 64, 128 * (i // 2) : 128 * (i // 2) + 128] if i < 8 else dout[64 * (i - 8) : 64 * (i - 8) + 64]
        send[pl.ds(8 + i, 64, stride=32), :] = source
        send[pl.ds(18 + i, 64, stride=32), :] = wgrad[64 * i : 64 * i + 64, :]
    for q in range(64):
        send[q * 32 + 28 : q * 32 + 32, :] = gb1


def fourth_kernel(recv, xin, dx_s, final_s, gain, shift, wbias, shares, tail):
    total = jnp.sum(recv[...].reshape(64, 32, 128), axis=0)
    x = jnp.concatenate([gather_rows(xin, (r * 128, r * 128 + 1), 2) for r in range(2)])
    unit, root = norm_parts(x)
    y = unit * gain[0:1, :] + shift[0:1, :]
    dy = jnp.concatenate([dot(total[4 * r : 4 * r + 4], wbias[0], 0, 0) for r in range(2)])
    gb0 = dot(total[0:4], y[:128], 1, 0) + dot(total[4:8], y[128:], 1, 0)
    dx = dx_s[...] + norm_back(dy, gain[0:1, :], unit, root)
    for r in range(2):
        scatter_rows(tail, (r * 128, r * 128 + 1), 2, dx[r * 128 : r * 128 + 128])
    tail[256:512, :] = final_s[...]
    tail[512:520, :] = jnp.concatenate([total[28:32], total[28:32]], axis=0) * (1.0 / 128)
    share = jnp.concatenate([total[8:28], gb0], axis=0) * (1.0 / 128)
    for k in range(4):
        shares[24 * k : 24 * k + 24, :] = share


def last_kernel(recv, gb1, gin, gbias, gout):
    for m in range(2):
        for i in range(10):
            piece = recv[pl.ds(10 * m + i, 64, stride=24), :]
            if i < 8:
                gin[m, 64 * (i % 2) : 64 * (i % 2) + 64, 128 * (i // 2) : 128 * (i // 2) + 128] = piece
            else:
                gout[m, 64 * (i - 8) : 64 * (i - 8) + 64, :] = piece
    gbias[0] = jnp.sum(recv[...].reshape(64, 24, 128), axis=0)[20:24]
    gbias[1] = gb1[0:4]


def call(kernel, outs, *args):
    return pl.pallas_call(
        kernel,
        out_shape=tuple(jax.ShapeDtypeStruct(s, f32) for s in outs),
        in_specs=[pl.BlockSpec(memory_space=pltpu.VMEM)] * len(args),
        out_specs=tuple(pl.BlockSpec(memory_space=pltpu.VMEM) for _ in outs),
        compiler_params=pltpu.CompilerParams(vmem_limit_bytes=48 * 1024 * 1024),
    )(*args)


def solution(mesh):
    placed, there, back, fours, planes = plans(mesh)

    def swap(a, groups):
        count = len(groups[0])
        cut = a.reshape(count, a.shape[0] // count, 128)
        got = lax.all_to_all(cut, both, 0, 0, axis_index_groups=groups, tiled=True)
        return got.reshape(a.shape)

    def body(pair, cotangent, gain, shift, win, wb, gate, wout):
        wbias = jnp.transpose(wb, (0, 2, 1))
        flat = jnp.concatenate([pair.reshape(256, 128), cotangent.reshape(256, 128)])
        xin = lax.ppermute(flat, both, there)
        (bsend,) = call(start_kernel, [(512, 128)], xin, gain, shift, wbias)
        brecv = swap(bsend, placed)
        send1, proj, probs, mixed, first = call(
            first_kernel,
            [(1024, 128), (256, 512), (1024, 128), (256, 128), (256, 128)],
            *(xin, brecv, gain, shift, win, wbias, gate, wout),
        )
        recv1 = swap(send1, placed)
        send2, wgrad = call(
            second_kernel, [(1024, 128), (640, 128)], recv1, gain, shift, win, gate, wout
        )
        recv2 = swap(send2, placed)
        send3, dx, final = call(
            third_kernel,
            [(2048, 128), (256, 128), (256, 128)],
            *(recv2, xin, first, proj, probs, mixed, wgrad, gain, shift, win, wbias, gate, wout),
        )
        recv3 = swap(send3, placed)
        shares, tail = call(
            fourth_kernel,
            [(96, 128), (520, 128)],
            *(recv3, xin, dx, final, gain, shift, wbias),
        )
        tail = lax.ppermute(tail, both, back)
        shares = lax.ppermute(swap(shares, fours), both, back)
        recv4 = swap(jnp.broadcast_to(shares[None], (16, 96, 128)).reshape(1536, 128), planes)
        gin, gbias, gout = call(
            last_kernel, [(2, 128, 512), (2, 4, 128), (2, 128, 128)], recv4, tail[512:520]
        )
        return (
            tail[256:512].reshape(2, 128, 128),
            tail[0:256].reshape(2, 128, 128),
            gin,
            jnp.transpose(gbias, (0, 2, 1)),
            gout,
        )

    rows = P(("dp", "axial"), None, None)
    part = P("dp", None, None)
    return jax.shard_map(
        body,
        mesh=mesh,
        in_specs=(rows, rows, P(), P(), P(), P(), P(), P()),
        out_specs=(rows, rows, part, part, part),
        check_vma=False,
    )
```

time: 2450 us -> 156 us (0.06)
  the two profiles are of different devices: /device:TPU:64 before, /device:TPU:66 now
where the time goes in v1:
time: 156 us
  blocking collectives  85.8 us (55%)
  waiting for transfers between devices  35.1 us (22%)
  starting transfers between devices  20 us (13%)
  Pallas kernels  10.9 us (7%)
  local copies, waits for them, and re-layouts  2.39 us (2%)
    all_to_all x5, blocking collectives, swap(): got = lax.all_to_all(cut, both, 0, 0, axis_index_groups=groups, tiled=True)  85.8 us
    ppermute x1, waiting for transfers between devices, body(): tail = lax.ppermute(tail, both, back)  18.2 us
    ppermute x1, starting transfers between devices, body(): xin = lax.ppermute(flat, both, there)  11.4 us
    pallas_call x6, Pallas kernels, call(): pl.pallas_call(kernel, out_shape=tuple((jax.ShapeDtypeStruct(s, f32) for...  10.9 us
    ppermute x1, waiting for transfers between devices, body(): shares = lax.ppermute(swap(shares, fours), both, back)  8.87 us
    ppermute x1, waiting for transfers between devices, body(): xin = lax.ppermute(flat, both, there)  8.08 us
    all_to_all x1, starting transfers between devices, swap(): got = lax.all_to_all(cut, both, 0, 0, axis_index_groups=groups, tiled=True)  4.76 us
  transfers between devices with their start and end apart: 4, of which 3 were waited for; matrix products, arithmetic and copies ran while one was open for 0% of the time, Pallas kernels for 0%

profile of v1, /device:TPU:66, one launch (start us, length us, event | category | flops | bytes accessed | tf_op | source)
XLA Modules:
  0.0 156.0 jit_solution(18332605546245131842)
XLA Ops:
  0.7 1.0 pad_maximum_fusion
  1.7 0.0 copy-start.3
  1.7 11.4 %collective-permute-start = (f32[512,128]{1,0:T(8,128)S(1)}, f32[512,128]{1,0:T(8,128)S(1)}, u32[]{:S(2)}, u32[]{:S(2)}) collective-permute-start(f32[512,128]{1,0:T(8,128)S(1)} %pad_maximum_fusion), channel_id=1, source_target_pairs={{0,386},{1,258},{2,322},{3,450},{4,390},{5,262},{6,326},{7,454},{8... | collective-permute-start | bytes 786440 | tf_op jit(solution)/shard_map/ppermute | solution.py:310
  13.1 8.1 %collective-permute-done.xin = f32[512,128]{1,0:T(8,128)S(1)} collective-permute-done((f32[512,128]{1,0:T(8,128)S(1)}, f32[512,128]{1,0:T(8,128)S(1)}, u32[]{:S(2)}, u32[]{:S(2)}) %collective-permute-start) | collective-permute-done | bytes 262176 | tf_op jit(solution)/shard_map/ppermute | solution.py:310
  21.1 0.4 shard_map.119
  21.6 0.0 copy-start.1
  21.6 23.1 %all_to_all.30 = f32[64,8,128]{2,1,0:T(8,128)S(1)} all-to-all(f32[64,8,128]{2,1,0:T(8,128)S(1)} %bitcast.22), channel_id=1, replica_groups={{386,258,322,450,390,262,326,454,394,266,330,458,398,270,334,462,402,27..., dimensions={0} | all-to-all | bytes 524288 | tf_op jit(solution)/shard_map/all_to_all | solution.py:304
  44.7 0.7 copy-done.5
  45.4 2.0 %shard_map.120 = (f32[1024,128]{1,0:T(8,128)S(1)}, f32[256,512]{1,0:T(8,128)S(1)}, f32[1024,128]{1,0:T(8,128)S(1)}, f32[256,128]{1,0:T(8,128)S(1)}, f32[256,128]{1,0:T(8,128)S(1)}) custom-call(f32[512,128]{1,0:T(8,128)S(1)} %collective-permute-done.xin, f32[512,128]{1,0:T(8,128)S(1)} %bitcast.23, f32[2,128]{1,0:T(2,128)S(1)} %copy-done.3, ...), custom_call_target="tpu_custom_call" | custom-call | tf_op jit(solution)/shard_map/pallas_call | solution.py:289
  47.4 16.9 %all_to_all.31 = f32[64,16,128]{2,1,0:T(8,128)S(1)} all-to-all(f32[64,16,128]{2,1,0:T(8,128)S(1)} %bitcast.24), channel_id=1, replica_groups={{386,258,322,450,390,262,326,454,394,266,330,458,398,270,334,462,402,27..., dimensions={0} | all-to-all | bytes 1048576 | tf_op jit(solution)/shard_map/all_to_all | solution.py:304
  64.3 3.7 %shard_map.121 = (f32[1024,128]{1,0:T(8,128)S(1)}, f32[640,128]{1,0:T(8,128)S(1)}) custom-call(f32[1024,128]{1,0:T(8,128)S(1)} %bitcast.20, f32[2,128]{1,0:T(2,128)S(1)} %copy-done.3, f32[2,128]{1,0:T(2,128)S(1)} %copy-done.4, f32[2,128,512]{2,1,0:T(8,128)S(1)} %copy-done, f32[2,128]{1,0:T(2,128)S(1)} %copy-done.5, f32[2,128,128]{2,1,0:T(8,128)S(1)} %copy-done.1), custom_call_target="tpu_custom_call" | custom-call | tf_op jit(solution)/shard_map/pallas_call | solution.py:289
  68.1 16.9 %all_to_all.32 = f32[64,16,128]{2,1,0:T(8,128)S(1)} all-to-all(f32[64,16,128]{2,1,0:T(8,128)S(1)} %bitcast.25), channel_id=1, replica_groups={{386,258,322,450,390,262,326,454,394,266,330,458,398,270,334,462,402,27..., dimensions={0} | all-to-all | bytes 1048576 | tf_op jit(solution)/shard_map/all_to_all | solution.py:304
  85.0 3.4 %shard_map.122 = (f32[2048,128]{1,0:T(8,128)S(1)}, f32[256,128]{1,0:T(8,128)S(1)}, f32[256,128]{1,0:T(8,128)S(1)}) custom-call(f32[1024,128]{1,0:T(8,128)S(1)} %bitcast.19, f32[512,128]{1,0:T(8,128)S(1)} %collective-permute-done.xin, f32[256,128]{1,0:T(8,128)S(1)} %get-tuple-element.22.first, f32[256,512]{1,0:T(8,128)S(1)} %get-tuple-element.23.proj_s, ...), custom_call_target="tpu_custom_call" | custom-call | tf_op jit(solution)/shard_map/pallas_call | solution.py:289
  88.4 22.6 %all_to_all.33 = f32[64,32,128]{2,1,0:T(8,128)S(1)} all-to-all(f32[64,32,128]{2,1,0:T(8,128)S(1)} %bitcast.21), channel_id=1, replica_groups={{386,258,322,450,390,262,326,454,394,266,330,458,398,270,334,462,402,27..., dimensions={0} | all-to-all | bytes 2097152 | tf_op jit(solution)/shard_map/all_to_all | solution.py:304
  110.9 0.5 shard_map.123
  111.4 6.3 %all_to_all.34 = f32[4,24,128]{2,1,0:T(8,128)S(1)} all-to-all(f32[4,24,128]{2,1,0:T(8,128)S(1)} %bitcast.30), channel_id=1, replica_groups={{386,258,322,450},{390,262,326,454},{394,266,330,458},{398,270,334,462}..., dimensions={0} | all-to-all | bytes 98304 | tf_op jit(solution)/shard_map/all_to_all | solution.py:304
  117.7 1.9 %collective-permute-start.2 = (f32[96,128]{1,0:T(8,128)S(1)}, f32[96,128]{1,0:T(8,128)S(1)}, u32[]{:S(2)}, u32[]{:S(2)}) collective-permute-start(f32[96,128]{1,0:T(8,128)S(1)} %bitcast.35), channel_id=1, source_target_pairs={{386,0},{258,1},{322,2},{450,3},{390,4},{262,5},{326,6},{454,7},{3... | collective-permute-start | bytes 147464 | tf_op jit(solution)/shard_map/ppermute | solution.py:335
  119.6 8.9 %collective-permute-done.2 = f32[96,128]{1,0:T(8,128)S(1)} collective-permute-done((f32[96,128]{1,0:T(8,128)S(1)}, f32[96,128]{1,0:T(8,128)S(1)}, u32[]{:S(2)}, u32[]{:S(2)}) %collective-permute-start.2) | collective-permute-done | bytes 49184 | tf_op jit(solution)/shard_map/ppermute | solution.py:335
  128.5 1.0 broadcast_in_dim.2
  129.5 4.8 %all-to-all-start.5 = ((f32[16,96,128]{2,1,0:T(8,128)}), f32[16,96,128]{2,1,0:T(8,128)S(1)}, u32[]{:S(2)}, u32[]{:S(2)}) async-start(f32[16,96,128]{2,1,0:T(8,128)} %broadcast_in_dim.2), calls=%async_computation.5 | async-start | bytes 1572864 | tf_op jit(solution)/shard_map/all_to_all | solution.py:304
  134.2 1.9 %collective-permute-start.1 = (f32[520,128]{1,0:T(8,128)S(1)}, f32[520,128]{1,0:T(8,128)S(1)}, u32[]{:S(2)}, u32[]{:S(2)}) collective-permute-start(f32[520,128]{1,0:T(8,128)S(1)} %get-tuple-element.30), channel_id=1, source_target_pairs={{386,0},{258,1},{322,2},{450,3},{390,4},{262,5},{326,6},{454,7},{3... | collective-permute-start | bytes 798728 | tf_op jit(solution)/shard_map/ppermute | solution.py:334
  136.1 18.2 %collective-permute-done.1 = f32[520,128]{1,0:T(8,128)S(1)} collective-permute-done((f32[520,128]{1,0:T(8,128)S(1)}, f32[520,128]{1,0:T(8,128)S(1)}, u32[]{:S(2)}, u32[]{:S(2)}) %collective-permute-start.1) | collective-permute-done | bytes 266272 | tf_op jit(solution)/shard_map/ppermute | solution.py:334
  154.3 0.7 fusion
  155.0 1.0 shard_map.124
  (11 shorter events, 0.0 us)
Async XLA Ops:
  0.6 20.5 %copy-start.2 = (f32[2,128,4]{1,2,0:T(4,128)S(1)}, f32[2,128,4]{1,2,0:T(4,128)}, u32[]{:S(2)}) copy-start(f32[2,128,4]{1,2,0:T(4,128)} %param.13) | copy-start | bytes 12292
  0.6 20.5 %copy-start.4 = (f32[2,128]{1,0:T(2,128)S(1)}, f32[2,128]{1,0:T(2,128)}, u32[]{:S(2)}) copy-start(f32[2,128]{1,0:T(2,128)} %shift.9) | copy-start | bytes 3076
  1.7 19.5 %copy-start.3 = (f32[2,128]{1,0:T(2,128)S(1)}, f32[2,128]{1,0:T(2,128)}, u32[]{:S(2)}) copy-start(f32[2,128]{1,0:T(2,128)} %gain.9) | copy-start | bytes 3076
  1.7 19.5 %collective-permute-start = (f32[512,128]{1,0:T(8,128)S(1)}, f32[512,128]{1,0:T(8,128)S(1)}, u32[]{:S(2)}, u32[]{:S(2)}) collective-permute-start(f32[512,128]{1,0:T(8,128)S(1)} %pad_maximum_fusion), channel_id=1, source_target_pairs={{0,386},{1,258},{2,322},{3,450},{4,390},{5,262},{6,326},{7,454},{8... | collective-permute-start | bytes 786440 | tf_op jit(solution)/shard_map/ppermute | solution.py:310
  21.1 23.6 %copy-start = (f32[2,128,512]{2,1,0:T(8,128)S(1)}, f32[2,128,512]{2,1,0:T(8,128)}, u32[]{:S(2)}) copy-start(f32[2,128,512]{2,1,0:T(8,128)} %win.5) | copy-start | bytes 1572868
  21.6 23.2 %copy-start.1 = (f32[2,128,128]{2,1,0:T(8,128)S(1)}, f32[2,128,128]{2,1,0:T(8,128)}, u32[]{:S(2)}) copy-start(f32[2,128,128]{2,1,0:T(8,128)} %wout.5) | copy-start | bytes 393220
  44.7 0.7 copy-start.5
  117.7 10.8 %collective-permute-start.2 = (f32[96,128]{1,0:T(8,128)S(1)}, f32[96,128]{1,0:T(8,128)S(1)}, u32[]{:S(2)}, u32[]{:S(2)}) collective-permute-start(f32[96,128]{1,0:T(8,128)S(1)} %bitcast.35), channel_id=1, source_target_pairs={{386,0},{258,1},{322,2},{450,3},{390,4},{262,5},{326,6},{454,7},{3... | collective-permute-start | bytes 147464 | tf_op jit(solution)/shard_map/ppermute | solution.py:335
  129.5 25.6 %all-to-all-start.5 = ((f32[16,96,128]{2,1,0:T(8,128)}), f32[16,96,128]{2,1,0:T(8,128)S(1)}, u32[]{:S(2)}, u32[]{:S(2)}) async-start(f32[16,96,128]{2,1,0:T(8,128)} %broadcast_in_dim.2), calls=%async_computation.5 | async-start | bytes 1572864 | tf_op jit(solution)/shard_map/all_to_all | solution.py:304
  134.2 20.1 %collective-permute-start.1 = (f32[520,128]{1,0:T(8,128)S(1)}, f32[520,128]{1,0:T(8,128)S(1)}, u32[]{:S(2)}, u32[]{:S(2)}) collective-permute-start(f32[520,128]{1,0:T(8,128)S(1)} %get-tuple-element.30), channel_id=1, source_target_pairs={{386,0},{258,1},{322,2},{450,3},{390,4},{262,5},{326,6},{454,7},{3... | collective-permute-start | bytes 798728 | tf_op jit(solution)/shard_map/ppermute | solution.py:334

commit v2 on v1

--- a/solution.py
+++ b/solution.py
@@ -118,7 +118,12 @@
     ref[pl.ds(b, 64, stride=stride), :] = value[64:]
 
 
-def start_kernel(xin, gain, shift, wbias, out):
+def vectors(small):
+    return small[0:2, :], small[2:4, :], small[4:6, :], (small[8:12, :], small[12:16, :])
+
+
+def start_kernel(xin, small, out):
+    gain, shift, _, wbias = vectors(small)
     rows = []
     for r in range(2):
         x = gather_rows(xin, (r * 128, r * 128 + 1), 2)
@@ -129,24 +134,33 @@
         out[q * 8 : q * 8 + 8, :] = block
 
 
-def first_kernel(
-    xin, brecv, gain, shift, win, wbias, gate, wout, send, proj_o, probs_o, mixed_o, first_o
-):
-    bias = jnp.concatenate([gather_rows(brecv, (h, 4 + h), 8) for h in range(4)])
+def project_kernel(xin, cot, small, win, x_o, proj_o, logits_o):
+    gain, shift, _, _ = vectors(small)
     x = jnp.concatenate([gather_rows(xin, (r * 128, r * 128 + 1), 2) for r in range(2)])
+    x_o[...] = x
     unit, root = norm_parts(x)
     proj = dot(unit * gain[0:1, :] + shift[0:1, :], win[0], 1, 0)
     proj_o[...] = proj
+    for r in range(2):
+        part = proj[r * 128 : r * 128 + 128]
+        logits_o[r * 512 : r * 512 + 512, :] = (
+            dot(by_head(part[:, 0:128]), part[:, 128:256], 1, 1) * SCALE
+        )
+
+
+def first_kernel(x, cot, brecv, proj, logits, small, wout, send, probs_o, mixed_o, first_o):
+    gain, shift, gate, wbias = vectors(small)
+    bias = jnp.concatenate([gather_rows(brecv, (h, 4 + h), 8) for h in range(4)])
     mixed = []
     for r in range(2):
-        part = proj[r * 128 : r * 128 + 128]
-        probs = probabilities(part[:, 0:128], part[:, 128:256], bias, False)
+        e = jnp.exp(logits[r * 512 : r * 512 + 512, :] + bias)
+        probs = e * (1.0 / jnp.sum(e, axis=1, keepdims=True))
         probs_o[r * 512 : r * 512 + 512, :] = probs
-        mixed.append(mix(probs, part[:, 256:384], False))
+        mixed.append(mix(probs, proj[r * 128 : r * 128 + 128, 256:384], False))
     mixed = jnp.concatenate(mixed)
     mixed_o[...] = mixed
     gated = jax.nn.sigmoid(proj[:, 384:512] + gate[0:1, :]) * mixed
-    first = x + dot(gated, wout[0], 1, 0)
+    first = x[...] + dot(gated, wout[0], 1, 0)
     first_o[...] = first
     unit1, root1 = norm_parts(first)
     y1 = unit1 * gain[1:2, :] + shift[1:2, :]
@@ -157,11 +171,12 @@
         send[q * 16 + 4 : q * 16 + 12, :] = bias_rows
     for r in range(2):
         scatter_rows(send, (r * 2, r * 2 + 1), 16, first[r * 128 : r * 128 + 128])
-        cot = gather_rows(xin, (256 + r * 128, 256 + r * 128 + 1), 2)
-        scatter_rows(send, (12 + r * 2, 12 + r * 2 + 1), 16, cot)
-
-
-def second_kernel(recv, gain, shift, win, gate, wout, send, wgrad):
+        rows = gather_rows(cot, (r * 128, r * 128 + 1), 2)
+        scatter_rows(send, (12 + r * 2, 12 + r * 2 + 1), 16, rows)
+
+
+def second_kernel(recv, small, win, wout, send, wgrad):
+    gain, shift, gate, _ = vectors(small)
     bias = jnp.concatenate([gather_rows(recv, (4 + h, 8 + h), 16) for h in range(4)])
     x = jnp.concatenate([gather_rows(recv, (c, 2 + c), 16) for c in range(2)])
     up = jnp.concatenate([gather_rows(recv, (12 + c, 14 + c), 16) for c in range(2)])
@@ -208,8 +223,9 @@
 
 
 def third_kernel(
-    recv, xin, first, proj_s, probs_s, mixed_s, wgrad, gain, shift, win, wbias, gate, wout, send, dx_o, final_o
+    recv, xin, first, proj_s, probs_s, mixed_s, wgrad, small, win, wout, send, dx_o, final_o
 ):
+    gain, shift, gate, wbias = vectors(small)
     for r in range(2):
         for c in range(2):
             final_o[pl.ds(r * 128 + c, 64, stride=2), :] = recv[pl.ds(12 + 2 * r + c, 64, stride=16), :]
@@ -220,8 +236,7 @@
     gb1 = dot(summed[0:4], y1[:128], 1, 0) + dot(summed[4:8], y1[128:], 1, 0)
     up = jnp.concatenate([gather_rows(recv, (2 * r, 2 * r + 1), 16) for r in range(2)])
     up = up + norm_back(dy1, gain[1:2, :], unit1, root1)
-    x = jnp.concatenate([gather_rows(xin, (r * 128, r * 128 + 1), 2) for r in range(2)])
-    unit, root = norm_parts(x)
+    unit, root = norm_parts(xin[...])
     y = unit * gain[0:1, :] + shift[0:1, :]
     proj = proj_s[...]
     mixed = mixed_s[...]
@@ -256,21 +271,28 @@
         send[q * 32 + 28 : q * 32 + 32, :] = gb1
 
 
-def fourth_kernel(recv, xin, dx_s, final_s, gain, shift, wbias, shares, tail):
+def fourth_kernel(recv, x, small, shares, totals):
+    gain, shift, _, _ = vectors(small)
     total = jnp.sum(recv[...].reshape(64, 32, 128), axis=0)
-    x = jnp.concatenate([gather_rows(xin, (r * 128, r * 128 + 1), 2) for r in range(2)])
-    unit, root = norm_parts(x)
+    unit, root = norm_parts(x[...])
     y = unit * gain[0:1, :] + shift[0:1, :]
-    dy = jnp.concatenate([dot(total[4 * r : 4 * r + 4], wbias[0], 0, 0) for r in range(2)])
     gb0 = dot(total[0:4], y[:128], 1, 0) + dot(total[4:8], y[128:], 1, 0)
-    dx = dx_s[...] + norm_back(dy, gain[0:1, :], unit, root)
-    for r in range(2):
-        scatter_rows(tail, (r * 128, r * 128 + 1), 2, dx[r * 128 : r * 128 + 128])
-    tail[256:512, :] = final_s[...]
-    tail[512:520, :] = jnp.concatenate([total[28:32], total[28:32]], axis=0) * (1.0 / 128)
+    totals[0:8, :] = total[0:8]
+    totals[8:16, :] = jnp.concatenate([total[28:32], total[28:32]], axis=0) * (1.0 / 128)
     share = jnp.concatenate([total[8:28], gb0], axis=0) * (1.0 / 128)
     for k in range(4):
         shares[24 * k : 24 * k + 24, :] = share
+
+
+def tail_kernel(shares, totals, x, dx_s, small, tail):
+    gain, _, _, wbias = vectors(small)
+    unit, root = norm_parts(x[...])
+    dy = jnp.concatenate([dot(totals[4 * r : 4 * r + 4, :], wbias[0], 0, 0) for r in range(2)])
+    dx = dx_s[...] + norm_back(dy, gain[0:1, :], unit, root)
+    for r in range(2):
+        scatter_rows(tail, (r * 128, r * 128 + 1), 2, dx[r * 128 : r * 128 + 128])
+    tail[256:352, :] = shares[...]
+    tail[352:360, :] = totals[8:16, :]
 
 
 def last_kernel(recv, gb1, gin, gbias, gout):
@@ -285,12 +307,13 @@
     gbias[1] = gb1[0:4]
 
 
-def call(kernel, outs, *args):
+def call(kernel, outs, *args, cost=None):
     return pl.pallas_call(
         kernel,
         out_shape=tuple(jax.ShapeDtypeStruct(s, f32) for s in outs),
         in_specs=[pl.BlockSpec(memory_space=pltpu.VMEM)] * len(args),
         out_specs=tuple(pl.BlockSpec(memory_space=pltpu.VMEM) for _ in outs),
+        cost_estimate=cost,
         compiler_params=pltpu.CompilerParams(vmem_limit_bytes=48 * 1024 * 1024),
     )(*args)
 
@@ -305,40 +328,52 @@
         return got.reshape(a.shape)
 
     def body(pair, cotangent, gain, shift, win, wb, gate, wout):
-        wbias = jnp.transpose(wb, (0, 2, 1))
-        flat = jnp.concatenate([pair.reshape(256, 128), cotangent.reshape(256, 128)])
-        xin = lax.ppermute(flat, both, there)
-        (bsend,) = call(start_kernel, [(512, 128)], xin, gain, shift, wbias)
+        wbias = jnp.transpose(wb, (0, 2, 1)).reshape(8, 128)
+        small = jnp.concatenate([gain, shift, gate, jnp.zeros_like(gate), wbias])
+        xin = lax.ppermute(pair.reshape(256, 128), both, there)
+        cot = lax.ppermute(cotangent.reshape(256, 128), both, there)
+        (bsend,) = call(start_kernel, [(512, 128)], xin, small)
         brecv = swap(bsend, placed)
-        send1, proj, probs, mixed, first = call(
+        x, proj, logits = call(
+            project_kernel,
+            [(256, 128), (256, 512), (1024, 128)],
+            *(xin, cot, small, win),
+            cost=pl.CostEstimate(flops=10**11, bytes_accessed=4 * 10**8, transcendentals=0),
+        )
+        send1, probs, mixed, first = call(
             first_kernel,
-            [(1024, 128), (256, 512), (1024, 128), (256, 128), (256, 128)],
-            *(xin, brecv, gain, shift, win, wbias, gate, wout),
+            [(1024, 128), (1024, 128), (256, 128), (256, 128)],
+            *(x, cot, brecv, proj, logits, small, wout),
         )
         recv1 = swap(send1, placed)
         send2, wgrad = call(
-            second_kernel, [(1024, 128), (640, 128)], recv1, gain, shift, win, gate, wout
+            second_kernel, [(1024, 128), (640, 128)], recv1, small, win, wout
         )
         recv2 = swap(send2, placed)
         send3, dx, final = call(
             third_kernel,
             [(2048, 128), (256, 128), (256, 128)],
-            *(recv2, xin, first, proj, probs, mixed, wgrad, gain, shift, win, wbias, gate, wout),
+            *(recv2, x, first, proj, probs, mixed, wgrad, small, win, wout),
         )
         recv3 = swap(send3, placed)
-        shares, tail = call(
-            fourth_kernel,
-            [(96, 128), (520, 128)],
-            *(recv3, xin, dx, final, gain, shift, wbias),
+        shares, totals = call(
+            fourth_kernel, [(96, 128), (16, 128)], recv3, x, small
+        )
+        (tail,) = call(
+            tail_kernel,
+            [(360, 128)],
+            *(swap(shares, fours), totals, x, dx, small),
         )
         tail = lax.ppermute(tail, both, back)
-        shares = lax.ppermute(swap(shares, fours), both, back)
-        recv4 = swap(jnp.broadcast_to(shares[None], (16, 96, 128)).reshape(1536, 128), planes)
+        final = lax.ppermute(final, both, back)
+        recv4 = swap(
+            jnp.broadcast_to(tail[None, 256:352], (16, 96, 128)).reshape(1536, 128), planes
+        )
         gin, gbias, gout = call(
-            last_kernel, [(2, 128, 512), (2, 4, 128), (2, 128, 128)], recv4, tail[512:520]
+            last_kernel, [(2, 128, 512), (2, 4, 128), (2, 128, 128)], recv4, tail[352:360]
         )
         return (
-            tail[256:512].reshape(2, 128, 128),
+            final.reshape(2, 128, 128),
             tail[0:256].reshape(2, 128, 128),
             gin,
             jnp.transpose(gbias, (0, 2, 1)),

time: 156 us -> 152 us (0.974)
  blocking collectives: 85.8 us -> 62.7 us
  starting transfers between devices: 20 us -> 37.4 us
    all_to_all x5 -> x4, blocking collectives: 85.8 us -> 62.7 us  [swap(): got = lax.all_to_all(cut, both, 0, 0, axis_index_groups=groups, tiled=True)]
    all_to_all x1 -> x2, starting transfers between devices: 4.76 us -> 18.6 us  [swap(): got = lax.all_to_all(cut, both, 0, 0, axis_index_groups=groups, tiled=True)]
    all_to_all x1 -> x2, waiting for transfers between devices: 0.01 us -> 8.15 us  [swap(): got = lax.all_to_all(cut, both, 0, 0, axis_index_groups=groups, tiled=True)]
    ppermute x2 -> x3, waiting for transfers between devices: 16.9 us -> 12.7 us  [the longest x1 11.1 us: body(): final = lax.ppermute(final, both, back)]
    ppermute x1, waiting for transfers between devices: 18.2 us -> 15 us  [body(): tail = lax.ppermute(tail, both, back)]
    ppermute x2 -> x3, starting transfers between devices: 13.3 us -> 15.3 us  [the longest x1 11.5 us: body(): xin = lax.ppermute(pair.reshape(256, 128), both, there)]
    pallas_call x6 -> x8, Pallas kernels: 10.9 us -> 11.9 us  [call(): pl.pallas_call(kernel, out_shape=tuple((jax.ShapeDtypeStruct(s, f32) for...]
  transfers between devices with their start and end apart: 4 -> 6, of which waited for: 3 -> 4; matrix products, arithmetic and copies ran while one was open for 0% -> 1% of each run, Pallas kernels for 0% -> 1%
where the time goes in v2:
time: 152 us
  blocking collectives  62.7 us (41%)
  starting transfers between devices  37.4 us (25%)
  waiting for transfers between devices  35.8 us (24%)
  Pallas kernels  11.9 us (8%)
  local copies, waits for them, and re-layouts  3.05 us (2%)
    all_to_all x4, blocking collectives, swap(): got = lax.all_to_all(cut, both, 0, 0, axis_index_groups=groups, tiled=True)  62.7 us
    all_to_all x2, starting transfers between devices, swap(): got = lax.all_to_all(cut, both, 0, 0, axis_index_groups=groups, tiled=True)  18.6 us
    ppermute x1, waiting for transfers between devices, body(): tail = lax.ppermute(tail, both, back)  15 us
    pallas_call x8, Pallas kernels, call(): pl.pallas_call(kernel, out_shape=tuple((jax.ShapeDtypeStruct(s, f32) for...  11.9 us
    ppermute x1, starting transfers between devices, body(): xin = lax.ppermute(pair.reshape(256, 128), both, there)  11.5 us
    ppermute x1, waiting for transfers between devices, body(): final = lax.ppermute(final, both, back)  11.1 us
    all_to_all x2, waiting for transfers between devices, swap(): got = lax.all_to_all(cut, both, 0, 0, axis_index_groups=groups, tiled=True)  8.15 us
    ppermute x1, starting transfers between devices, body(): tail = lax.ppermute(tail, both, back)  3.39 us
  transfers between devices with their start and end apart: 6, of which 4 were waited for; matrix products, arithmetic and copies ran while one was open for 1% of the time, Pallas kernels for 1%

profile of v2, /device:TPU:66, one launch (start us, length us, event | category | flops | bytes accessed | tf_op | source)
XLA Modules:
  0.0 151.6 jit_solution(55267265954786678)
XLA Ops:
  0.7 11.5 %collective-permute-start = (f32[256,128]{1,0:T(8,128)}, f32[256,128]{1,0:T(8,128)S(1)}, u32[]{:S(2)}, u32[]{:S(2)}) collective-permute-start(f32[256,128]{1,0:T(8,128)} %bitcast.32), channel_id=1, source_target_pairs={{0,386},{1,258},{2,322},{3,450},{4,390},{5,262},{6,326},{7,454},{8... | collective-permute-start | bytes 393224 | tf_op jit(solution)/shard_map/ppermute | solution.py:333
  12.2 1.9 %collective-permute-start.1 = (f32[256,128]{1,0:T(8,128)}, f32[256,128]{1,0:T(8,128)S(1)}, u32[]{:S(2)}, u32[]{:S(2)}) collective-permute-start(f32[256,128]{1,0:T(8,128)} %bitcast.33), channel_id=1, source_target_pairs={{0,386},{1,258},{2,322},{3,450},{4,390},{5,262},{6,326},{7,454},{8... | collective-permute-start | bytes 393224 | tf_op jit(solution)/shard_map/ppermute | solution.py:334
  14.1 0.7 concatenate.3.small
  14.9 1.5 %collective-permute-done.xin = f32[256,128]{1,0:T(8,128)S(1)} collective-permute-done((f32[256,128]{1,0:T(8,128)}, f32[256,128]{1,0:T(8,128)S(1)}, u32[]{:S(2)}, u32[]{:S(2)}) %collective-permute-start) | collective-permute-done | bytes 131104 | tf_op jit(solution)/shard_map/ppermute | solution.py:333
  16.4 1.1 shard_map.120
  17.5 13.9 %all-to-all-start = ((f32[64,8,128]{2,1,0:T(8,128)}), f32[64,8,128]{2,1,0:T(8,128)S(1)}, u32[]{:S(2)}, u32[]{:S(2)}) async-start(f32[64,8,128]{2,1,0:T(8,128)} %bitcast.4), calls=%async_computation | async-start | bytes 524288 | tf_op jit(solution)/shard_map/all_to_all | solution.py:327
  31.4 0.8 shard_map.119
  32.3 8.1 %all-to-all-done = f32[64,8,128]{2,1,0:T(8,128)S(1)} async-done(((f32[64,8,128]{2,1,0:T(8,128)}), f32[64,8,128]{2,1,0:T(8,128)S(1)}, u32[]{:S(2)}, u32[]{:S(2)}) %all-to-all-start) | async-done | bytes 262176 | tf_op jit(solution)/shard_map/all_to_all | solution.py:327
  40.4 1.1 shard_map.121
  41.5 17.0 %all_to_all.30 = f32[64,16,128]{2,1,0:T(8,128)S(1)} all-to-all(f32[64,16,128]{2,1,0:T(8,128)S(1)} %bitcast.25), channel_id=1, replica_groups={{386,258,322,450,390,262,326,454,394,266,330,458,398,270,334,462,402,27..., dimensions={0} | all-to-all | bytes 1048576 | tf_op jit(solution)/shard_map/all_to_all | solution.py:327
  58.5 3.7 %shard_map.122 = (f32[1024,128]{1,0:T(8,128)S(1)}, f32[640,128]{1,0:T(8,128)S(1)}) custom-call(f32[1024,128]{1,0:T(8,128)S(1)} %bitcast.21, f32[16,128]{1,0:T(8,128)S(1)} %concatenate.3.small, f32[2,128,512]{2,1,0:T(8,128)S(1)} %copy-done, f32[2,128,128]{2,1,0:T(8,128)S(1)} %copy-done.1), custom_call_target="tpu_custom_call" | custom-call | tf_op jit(solution)/shard_map/pallas_call | solution.py:311
  62.2 16.9 %all_to_all.31 = f32[64,16,128]{2,1,0:T(8,128)S(1)} all-to-all(f32[64,16,128]{2,1,0:T(8,128)S(1)} %bitcast.26), channel_id=1, replica_groups={{386,258,322,450,390,262,326,454,394,266,330,458,398,270,334,462,402,27..., dimensions={0} | all-to-all | bytes 1048576 | tf_op jit(solution)/shard_map/all_to_all | solution.py:327
  79.1 3.4 %shard_map.123 = (f32[2048,128]{1,0:T(8,128)S(1)}, f32[256,128]{1,0:T(8,128)S(1)}, f32[256,128]{1,0:T(8,128)S(1)}) custom-call(f32[1024,128]{1,0:T(8,128)S(1)} %bitcast.22, f32[256,128]{1,0:T(8,128)S(1)} %get-tuple-element.22.x.xin, f32[256,128]{1,0:T(8,128)S(1)} %get-tuple-element.27.first, f32[256,512]{1,0:T(8,128)S(1)} %get-tuple-element.23.proj.proj_s, ...), custom_call_target="tpu_custom_call" | custom-call | tf_op jit(solution)/shard_map/pallas_call | solution.py:311
  82.5 22.6 %all_to_all.32 = f32[64,32,128]{2,1,0:T(8,128)S(1)} all-to-all(f32[64,32,128]{2,1,0:T(8,128)S(1)} %bitcast.23), channel_id=1, replica_groups={{386,258,322,450,390,262,326,454,394,266,330,458,398,270,334,462,402,27..., dimensions={0} | all-to-all | bytes 2097152 | tf_op jit(solution)/shard_map/all_to_all | solution.py:327
  105.4 6.3 %all_to_all.33 = f32[4,24,128]{2,1,0:T(8,128)S(1)} all-to-all(f32[4,24,128]{2,1,0:T(8,128)S(1)} %bitcast.28), channel_id=1, replica_groups={{386,258,322,450},{390,262,326,454},{394,266,330,458},{398,270,334,462}..., dimensions={0} | all-to-all | bytes 98304 | tf_op jit(solution)/shard_map/all_to_all | solution.py:327
  112.1 3.4 %collective-permute-start.3 = (f32[360,128]{1,0:T(8,128)S(1)}, f32[360,128]{1,0:T(8,128)S(1)}, u32[]{:S(2)}, u32[]{:S(2)}) collective-permute-start(f32[360,128]{1,0:T(8,128)S(1)} %shard_map.125), channel_id=1, source_target_pairs={{386,0},{258,1},{322,2},{450,3},{390,4},{262,5},{326,6},{454,7},{3... | collective-permute-start | bytes 552968 | tf_op jit(solution)/shard_map/ppermute | solution.py:367
  115.5 15.0 %collective-permute-done.3 = f32[360,128]{1,0:T(8,128)S(1)} collective-permute-done((f32[360,128]{1,0:T(8,128)S(1)}, f32[360,128]{1,0:T(8,128)S(1)}, u32[]{:S(2)}, u32[]{:S(2)}) %collective-permute-start.3) | collective-permute-done | bytes 184352 | tf_op jit(solution)/shard_map/ppermute | solution.py:367
  130.5 1.0 broadcast_in_dim.10
  131.5 4.8 %all-to-all-start.5 = ((f32[16,96,128]{2,1,0:T(8,128)}), f32[16,96,128]{2,1,0:T(8,128)S(1)}, u32[]{:S(2)}, u32[]{:S(2)}) async-start(f32[16,96,128]{2,1,0:T(8,128)} %broadcast_in_dim.10), calls=%async_computation.5 | async-start | bytes 1572864 | tf_op jit(solution)/shard_map/all_to_all | solution.py:327
  136.2 1.9 %collective-permute-start.2 = (f32[256,128]{1,0:T(8,128)S(1)}, f32[256,128]{1,0:T(8,128)S(1)}, u32[]{:S(2)}, u32[]{:S(2)}) collective-permute-start(f32[256,128]{1,0:T(8,128)S(1)} %get-tuple-element.31), channel_id=1, source_target_pairs={{386,0},{258,1},{322,2},{450,3},{390,4},{262,5},{326,6},{454,7},{3... | collective-permute-start | bytes 393224 | tf_op jit(solution)/shard_map/ppermute | solution.py:368
  138.1 11.1 %collective-permute-done.2 = f32[256,128]{1,0:T(8,128)S(1)} collective-permute-done((f32[256,128]{1,0:T(8,128)S(1)}, f32[256,128]{1,0:T(8,128)S(1)}, u32[]{:S(2)}, u32[]{:S(2)}) %collective-permute-start.2) | collective-permute-done | bytes 131104 | tf_op jit(solution)/shard_map/ppermute | solution.py:368
  149.3 0.7 slice.12
  150.0 1.0 shard_map.126
  150.9 0.7 copy.14
  (13 shorter events, 0.8 us)
Async XLA Ops:
  0.6 13.5 %copy-start.2 = (f32[2,128,4]{1,2,0:T(4,128)S(1)}, f32[2,128,4]{1,2,0:T(4,128)}, u32[]{:S(2)}) copy-start(f32[2,128,4]{1,2,0:T(4,128)} %param.13) | copy-start | bytes 12292
  0.6 30.8 %copy-start = (f32[2,128,512]{2,1,0:T(8,128)S(1)}, f32[2,128,512]{2,1,0:T(8,128)}, u32[]{:S(2)}) copy-start(f32[2,128,512]{2,1,0:T(8,128)} %win.5) | copy-start | bytes 1572868
  0.7 15.7 %collective-permute-start = (f32[256,128]{1,0:T(8,128)}, f32[256,128]{1,0:T(8,128)S(1)}, u32[]{:S(2)}, u32[]{:S(2)}) collective-permute-start(f32[256,128]{1,0:T(8,128)} %bitcast.32), channel_id=1, source_target_pairs={{0,386},{1,258},{2,322},{3,450},{4,390},{5,262},{6,326},{7,454},{8... | collective-permute-start | bytes 393224 | tf_op jit(solution)/shard_map/ppermute | solution.py:333
  12.2 19.2 %collective-permute-start.1 = (f32[256,128]{1,0:T(8,128)}, f32[256,128]{1,0:T(8,128)S(1)}, u32[]{:S(2)}, u32[]{:S(2)}) collective-permute-start(f32[256,128]{1,0:T(8,128)} %bitcast.33), channel_id=1, source_target_pairs={{0,386},{1,258},{2,322},{3,450},{4,390},{5,262},{6,326},{7,454},{8... | collective-permute-start | bytes 393224 | tf_op jit(solution)/shard_map/ppermute | solution.py:334
  17.5 22.9 %all-to-all-start = ((f32[64,8,128]{2,1,0:T(8,128)}), f32[64,8,128]{2,1,0:T(8,128)S(1)}, u32[]{:S(2)}, u32[]{:S(2)}) async-start(f32[64,8,128]{2,1,0:T(8,128)} %bitcast.4), calls=%async_computation | async-start | bytes 524288 | tf_op jit(solution)/shard_map/all_to_all | solution.py:327
  31.4 9.0 %copy-start.1 = (f32[2,128,128]{2,1,0:T(8,128)S(1)}, f32[2,128,128]{2,1,0:T(8,128)}, u32[]{:S(2)}) copy-start(f32[2,128,128]{2,1,0:T(8,128)} %wout.5) | copy-start | bytes 393220
  112.1 18.4 %collective-permute-start.3 = (f32[360,128]{1,0:T(8,128)S(1)}, f32[360,128]{1,0:T(8,128)S(1)}, u32[]{:S(2)}, u32[]{:S(2)}) collective-permute-start(f32[360,128]{1,0:T(8,128)S(1)} %shard_map.125), channel_id=1, source_target_pairs={{386,0},{258,1},{322,2},{450,3},{390,4},{262,5},{326,6},{454,7},{3... | collective-permute-start | bytes 552968 | tf_op jit(solution)/shard_map/ppermute | solution.py:367
  131.5 18.5 %all-to-all-start.5 = ((f32[16,96,128]{2,1,0:T(8,128)}), f32[16,96,128]{2,1,0:T(8,128)S(1)}, u32[]{:S(2)}, u32[]{:S(2)}) async-start(f32[16,96,128]{2,1,0:T(8,128)} %broadcast_in_dim.10), calls=%async_computation.5 | async-start | bytes 1572864 | tf_op jit(solution)/shard_map/all_to_all | solution.py:327
  136.2 13.1 %collective-permute-start.2 = (f32[256,128]{1,0:T(8,128)S(1)}, f32[256,128]{1,0:T(8,128)S(1)}, u32[]{:S(2)}, u32[]{:S(2)}) collective-permute-start(f32[256,128]{1,0:T(8,128)S(1)} %get-tuple-element.31), channel_id=1, source_target_pairs={{386,0},{258,1},{322,2},{450,3},{390,4},{262,5},{326,6},{454,7},{3... | collective-permute-start | bytes 393224 | tf_op jit(solution)/shard_map/ppermute | solution.py:368

commit v3 on v2

--- a/solution.py
+++ b/solution.py
@@ -70,6 +70,7 @@
 
 
 SCALE = 32**-0.5
+LONG = pl.CostEstimate(flops=10**11, bytes_accessed=4 * 10**8, transcendentals=0)
 
 
 def probabilities(q, k, bias, keys_down):
@@ -223,7 +224,7 @@
 
 
 def third_kernel(
-    recv, xin, first, proj_s, probs_s, mixed_s, wgrad, small, win, wout, send, dx_o, final_o
+    recv, xin, first, proj_s, probs_s, mixed_s, wgrad, small, win, wout, send, dx_o, final_o, gb1_o
 ):
     gain, shift, gate, wbias = vectors(small)
     for r in range(2):
@@ -262,26 +263,26 @@
     din = dot(y, dproj, 0, 0)
     dx_o[...] = up + norm_back(dot(dproj, win[0], 1, 1), gain[0:1, :], unit, root)
     for h in range(4):
-        scatter_rows(send, (h, 4 + h), 32, dbias[h * 128 : h * 128 + 128])
+        scatter_rows(send, (h, 4 + h), 28, dbias[h * 128 : h * 128 + 128])
     for i in range(10):
         source = din[64 * (i % 2) : 64 * (i % 2) + 64, 128 * (i // 2) : 128 * (i // 2) + 128] if i < 8 else dout[64 * (i - 8) : 64 * (i - 8) + 64]
-        send[pl.ds(8 + i, 64, stride=32), :] = source
-        send[pl.ds(18 + i, 64, stride=32), :] = wgrad[64 * i : 64 * i + 64, :]
-    for q in range(64):
-        send[q * 32 + 28 : q * 32 + 32, :] = gb1
-
-
-def fourth_kernel(recv, x, small, shares, totals):
+        send[pl.ds(8 + i, 64, stride=28), :] = source
+        send[pl.ds(18 + i, 64, stride=28), :] = wgrad[64 * i : 64 * i + 64, :]
+    gb1_o[0:4, :] = gb1
+    gb1_o[4:8, :] = gb1
+
+
+def fourth_kernel(recv, x, gb1, small, shares, totals):
     gain, shift, _, _ = vectors(small)
-    total = jnp.sum(recv[...].reshape(64, 32, 128), axis=0)
+    pair_sum = jnp.sum(recv[...].reshape(32, 56, 128), axis=0)
+    total = pair_sum[0:28] + pair_sum[28:56]
     unit, root = norm_parts(x[...])
     y = unit * gain[0:1, :] + shift[0:1, :]
     gb0 = dot(total[0:4], y[:128], 1, 0) + dot(total[4:8], y[128:], 1, 0)
-    totals[0:8, :] = total[0:8]
-    totals[8:16, :] = jnp.concatenate([total[28:32], total[28:32]], axis=0) * (1.0 / 128)
-    share = jnp.concatenate([total[8:28], gb0], axis=0) * (1.0 / 128)
+    totals[...] = total[0:8]
+    share = jnp.concatenate([total[8:28], gb0, gb1[0:4, :], jnp.zeros((4, 128), f32)], axis=0) * (1.0 / 128)
     for k in range(4):
-        shares[24 * k : 24 * k + 24, :] = share
+        shares[32 * k : 32 * k + 32, :] = share
 
 
 def tail_kernel(shares, totals, x, dx_s, small, tail):
@@ -291,28 +292,34 @@
     dx = dx_s[...] + norm_back(dy, gain[0:1, :], unit, root)
     for r in range(2):
         scatter_rows(tail, (r * 128, r * 128 + 1), 2, dx[r * 128 : r * 128 + 128])
-    tail[256:352, :] = shares[...]
-    tail[352:360, :] = totals[8:16, :]
-
-
-def last_kernel(recv, gb1, gin, gbias, gout):
+    for k in range(4):
+        tail[256 + 20 * k : 276 + 20 * k, :] = shares[32 * k : 32 * k + 20, :]
+    tail[336:344, :] = jnp.sum(shares[...].reshape(4, 32, 128)[:, 20:28, :], axis=0)
+
+
+def last_kernel(recv, tail, final, gin, gbias, gout, grad_o, final_o, rows):
+    for j in range(20):
+        for k in range(4):
+            rows[pl.ds(64 * j + k, 16, stride=4), :] = recv[pl.ds(20 * k + j, 16, stride=88), :]
     for m in range(2):
-        for i in range(10):
-            piece = recv[pl.ds(10 * m + i, 64, stride=24), :]
-            if i < 8:
-                gin[m, 64 * (i % 2) : 64 * (i % 2) + 64, 128 * (i // 2) : 128 * (i // 2) + 128] = piece
-            else:
-                gout[m, 64 * (i - 8) : 64 * (i - 8) + 64, :] = piece
-    gbias[0] = jnp.sum(recv[...].reshape(64, 24, 128), axis=0)[20:24]
-    gbias[1] = gb1[0:4]
-
-
-def call(kernel, outs, *args, cost=None):
+        for e in range(4):
+            first = 640 * m + 128 * e
+            gin[m, :, 128 * e : 128 * e + 128] = rows[first : first + 128, :]
+        gout[m] = rows[640 * m + 512 : 640 * m + 640, :]
+    both_bias = jnp.sum(recv[...].reshape(16, 88, 128), axis=0)[80:88]
+    gbias[0] = both_bias[0:4]
+    gbias[1] = both_bias[4:8]
+    grad_o[...] = tail[0:256, :]
+    final_o[...] = final[...]
+
+
+def call(kernel, outs, *args, cost=None, scratch=()):
     return pl.pallas_call(
         kernel,
         out_shape=tuple(jax.ShapeDtypeStruct(s, f32) for s in outs),
         in_specs=[pl.BlockSpec(memory_space=pltpu.VMEM)] * len(args),
         out_specs=tuple(pl.BlockSpec(memory_space=pltpu.VMEM) for _ in outs),
+        scratch_shapes=scratch,
         cost_estimate=cost,
         compiler_params=pltpu.CompilerParams(vmem_limit_bytes=48 * 1024 * 1024),
     )(*args)
@@ -322,8 +329,9 @@
     placed, there, back, fours, planes = plans(mesh)
 
     def swap(a, groups):
-        count = len(groups[0])
-        cut = a.reshape(count, a.shape[0] // count, 128)
+        each = a.shape[0] // len(groups[0])
+        tile = 8 if each % 8 == 0 else 4
+        cut = a.reshape(a.shape[0] // tile, tile, 128) if tile == 4 else a.reshape(-1, each, 128)
         got = lax.all_to_all(cut, both, 0, 0, axis_index_groups=groups, tiled=True)
         return got.reshape(a.shape)
 
@@ -338,7 +346,7 @@
             project_kernel,
             [(256, 128), (256, 512), (1024, 128)],
             *(xin, cot, small, win),
-            cost=pl.CostEstimate(flops=10**11, bytes_accessed=4 * 10**8, transcendentals=0),
+            cost=LONG,
         )
         send1, probs, mixed, first = call(
             first_kernel,
@@ -350,31 +358,34 @@
             second_kernel, [(1024, 128), (640, 128)], recv1, small, win, wout
         )
         recv2 = swap(send2, placed)
-        send3, dx, final = call(
+        send3, dx, final, gb1 = call(
             third_kernel,
-            [(2048, 128), (256, 128), (256, 128)],
+            [(1792, 128), (256, 128), (256, 128), (8, 128)],
             *(recv2, x, first, proj, probs, mixed, wgrad, small, win, wout),
         )
         recv3 = swap(send3, placed)
         shares, totals = call(
-            fourth_kernel, [(96, 128), (16, 128)], recv3, x, small
+            fourth_kernel, [(128, 128), (8, 128)], recv3, x, gb1, small
         )
         (tail,) = call(
             tail_kernel,
-            [(360, 128)],
+            [(344, 128)],
             *(swap(shares, fours), totals, x, dx, small),
         )
         tail = lax.ppermute(tail, both, back)
         final = lax.ppermute(final, both, back)
         recv4 = swap(
-            jnp.broadcast_to(tail[None, 256:352], (16, 96, 128)).reshape(1536, 128), planes
-        )
-        gin, gbias, gout = call(
-            last_kernel, [(2, 128, 512), (2, 4, 128), (2, 128, 128)], recv4, tail[352:360]
+            jnp.broadcast_to(tail[None, 256:344], (16, 88, 128)).reshape(1408, 128), planes
+        )
+        gin, gbias, gout, grad, final = call(
+            last_kernel,
+            [(2, 128, 512), (2, 4, 128), (2, 128, 128), (256, 128), (256, 128)],
+            *(recv4, tail, final),
+            scratch=[pltpu.VMEM((1280, 128), f32)],
         )
         return (
             final.reshape(2, 128, 128),
-            tail[0:256].reshape(2, 128, 128),
+            grad.reshape(2, 128, 128),
             gin,
             jnp.transpose(gbias, (0, 2, 1)),
             gout,

time: 152 us -> 149 us (0.980)
  transfers between devices with their start and end apart: 6 -> 6, of which waited for: 4 -> 4; matrix products, arithmetic and copies ran while one was open for 1% -> 0% of each run, Pallas kernels for 1% -> 1%
where the time goes in v3:
time: 149 us; the launch traced here: 148 us
  blocking collectives  61.3 us (41%)
  starting transfers between devices  37.5 us (25%)
  waiting for transfers between devices  35.3 us (24%)
  Pallas kernels  11.4 us (8%)
  local copies, waits for them, and re-layouts  1.67 us (1%)
    all_to_all x4, blocking collectives, swap(): got = lax.all_to_all(cut, both, 0, 0, axis_index_groups=groups, tiled=True)  61.3 us
    all_to_all x2, starting transfers between devices, swap(): got = lax.all_to_all(cut, both, 0, 0, axis_index_groups=groups, tiled=True)  18.6 us
    ppermute x1, waiting for transfers between devices, body(): tail = lax.ppermute(tail, both, back)  14.5 us
    ppermute x1, starting transfers between devices, body(): xin = lax.ppermute(pair.reshape(256, 128), both, there)  11.5 us
    pallas_call x8, Pallas kernels, call(): pl.pallas_call(kernel, out_shape=tuple((jax.ShapeDtypeStruct(s, f32) for...  11.4 us
    ppermute x1, waiting for transfers between devices, body(): final = lax.ppermute(final, both, back)  11.1 us
    all_to_all x2, waiting for transfers between devices, swap(): got = lax.all_to_all(cut, both, 0, 0, axis_index_groups=groups, tiled=True)  8.15 us
    ppermute x1, starting transfers between devices, body(): tail = lax.ppermute(tail, both, back)  3.56 us
  transfers between devices with their start and end apart: 6, of which 4 were waited for; matrix products, arithmetic and copies ran while one was open for 0% of the time, Pallas kernels for 1%

profile of v3, /device:TPU:66, one launch (start us, length us, event | category | flops | bytes accessed | tf_op | source)
XLA Modules:
  0.0 148.0 jit_solution(10615972471832303143)
XLA Ops:
  0.7 11.5 %collective-permute-start = (f32[256,128]{1,0:T(8,128)}, f32[256,128]{1,0:T(8,128)S(1)}, u32[]{:S(2)}, u32[]{:S(2)}) collective-permute-start(f32[256,128]{1,0:T(8,128)} %bitcast.30), channel_id=1, source_target_pairs={{0,386},{1,258},{2,322},{3,450},{4,390},{5,262},{6,326},{7,454},{8... | collective-permute-start | bytes 393224 | tf_op jit(solution)/shard_map/ppermute | solution.py:341
  12.2 1.9 %collective-permute-start.1 = (f32[256,128]{1,0:T(8,128)}, f32[256,128]{1,0:T(8,128)S(1)}, u32[]{:S(2)}, u32[]{:S(2)}) collective-permute-start(f32[256,128]{1,0:T(8,128)} %bitcast.31), channel_id=1, source_target_pairs={{0,386},{1,258},{2,322},{3,450},{4,390},{5,262},{6,326},{7,454},{8... | collective-permute-start | bytes 393224 | tf_op jit(solution)/shard_map/ppermute | solution.py:342
  14.1 0.7 concatenate.3.small
  14.9 1.5 %collective-permute-done.xin = f32[256,128]{1,0:T(8,128)S(1)} collective-permute-done((f32[256,128]{1,0:T(8,128)}, f32[256,128]{1,0:T(8,128)S(1)}, u32[]{:S(2)}, u32[]{:S(2)}) %collective-permute-start) | collective-permute-done | bytes 131104 | tf_op jit(solution)/shard_map/ppermute | solution.py:341
  16.4 1.1 shard_map.120
  17.5 13.9 %all-to-all-start = ((f32[64,8,128]{2,1,0:T(8,128)}), f32[64,8,128]{2,1,0:T(8,128)S(1)}, u32[]{:S(2)}, u32[]{:S(2)}) async-start(f32[64,8,128]{2,1,0:T(8,128)} %bitcast.4), calls=%async_computation | async-start | bytes 524288 | tf_op jit(solution)/shard_map/all_to_all | solution.py:335
  31.4 0.8 shard_map.119
  32.2 8.1 %all-to-all-done = f32[64,8,128]{2,1,0:T(8,128)S(1)} async-done(((f32[64,8,128]{2,1,0:T(8,128)}), f32[64,8,128]{2,1,0:T(8,128)S(1)}, u32[]{:S(2)}, u32[]{:S(2)}) %all-to-all-start) | async-done | bytes 262176 | tf_op jit(solution)/shard_map/all_to_all | solution.py:335
  40.4 1.1 shard_map.121
  41.5 17.0 %all_to_all.30 = f32[64,16,128]{2,1,0:T(8,128)S(1)} all-to-all(f32[64,16,128]{2,1,0:T(8,128)S(1)} %bitcast.25), channel_id=1, replica_groups={{386,258,322,450,390,262,326,454,394,266,330,458,398,270,334,462,402,27..., dimensions={0} | all-to-all | bytes 1048576 | tf_op jit(solution)/shard_map/all_to_all | solution.py:335
  58.5 3.7 %shard_map.122 = (f32[1024,128]{1,0:T(8,128)S(1)}, f32[640,128]{1,0:T(8,128)S(1)}) custom-call(f32[1024,128]{1,0:T(8,128)S(1)} %bitcast.21, f32[16,128]{1,0:T(8,128)S(1)} %concatenate.3.small, f32[2,128,512]{2,1,0:T(8,128)S(1)} %copy-done, f32[2,128,128]{2,1,0:T(8,128)S(1)} %copy-done.1), custom_call_target="tpu_custom_call" | custom-call | tf_op jit(solution)/shard_map/pallas_call | solution.py:317
  62.2 16.9 %all_to_all.31 = f32[64,16,128]{2,1,0:T(8,128)S(1)} all-to-all(f32[64,16,128]{2,1,0:T(8,128)S(1)} %bitcast.26), channel_id=1, replica_groups={{386,258,322,450,390,262,326,454,394,266,330,458,398,270,334,462,402,27..., dimensions={0} | all-to-all | bytes 1048576 | tf_op jit(solution)/shard_map/all_to_all | solution.py:335
  79.1 2.8 %shard_map.123 = (f32[1792,128]{1,0:T(8,128)S(1)}, f32[256,128]{1,0:T(8,128)S(1)}, f32[256,128]{1,0:T(8,128)S(1)}, f32[8,128]{1,0:T(8,128)S(1)}) custom-call(f32[1024,128]{1,0:T(8,128)S(1)} %bitcast.22, f32[256,128]{1,0:T(8,128)S(1)} %get-tuple-element.25.x.xin, f32[256,128]{1,0:T(8,128)S(1)} %get-tuple-element.30.first, ...), custom_call_target="tpu_custom_call" | custom-call | tf_op jit(solution)/shard_map/pallas_call | solution.py:317
  81.9 21.1 %all_to_all.32 = f32[448,4,128]{2,1,0:T(4,128)S(1)} all-to-all(f32[448,4,128]{2,1,0:T(4,128)S(1)} %bitcast.24), channel_id=1, replica_groups={{386,258,322,450,390,262,326,454,394,266,330,458,398,270,334,462,402,27..., dimensions={0} | all-to-all | bytes 1835008 | tf_op jit(solution)/shard_map/all_to_all | solution.py:335
  103.1 0.3 shard_map.124
  103.4 6.3 %all_to_all.33 = f32[4,32,128]{2,1,0:T(8,128)S(1)} all-to-all(f32[4,32,128]{2,1,0:T(8,128)S(1)} %bitcast.28), channel_id=1, replica_groups={{386,258,322,450},{390,262,326,454},{394,266,330,458},{398,270,334,462}..., dimensions={0} | all-to-all | bytes 131072 | tf_op jit(solution)/shard_map/all_to_all | solution.py:335
  109.7 0.4 shard_map.125
  110.2 3.6 %collective-permute-start.2 = (f32[344,128]{1,0:T(8,128)S(1)}, f32[344,128]{1,0:T(8,128)S(1)}, u32[]{:S(2)}, u32[]{:S(2)}) collective-permute-start(f32[344,128]{1,0:T(8,128)S(1)} %shard_map.125), channel_id=1, source_target_pairs={{386,0},{258,1},{322,2},{450,3},{390,4},{262,5},{326,6},{454,7},{3... | collective-permute-start | bytes 528392 | tf_op jit(solution)/shard_map/ppermute | solution.py:375
  113.7 14.5 %collective-permute-done.2.tail = f32[344,128]{1,0:T(8,128)S(1)} collective-permute-done((f32[344,128]{1,0:T(8,128)S(1)}, f32[344,128]{1,0:T(8,128)S(1)}, u32[]{:S(2)}, u32[]{:S(2)}) %collective-permute-start.2) | collective-permute-done | bytes 176160 | tf_op jit(solution)/shard_map/ppermute | solution.py:375
  128.2 0.9 broadcast_in_dim.10
  129.1 4.8 %all-to-all-start.5 = ((f32[16,88,128]{2,1,0:T(8,128)}), f32[16,88,128]{2,1,0:T(8,128)S(1)}, u32[]{:S(2)}, u32[]{:S(2)}) async-start(f32[16,88,128]{2,1,0:T(8,128)} %broadcast_in_dim.10), calls=%async_computation.5 | async-start | bytes 1441792 | tf_op jit(solution)/shard_map/all_to_all | solution.py:335
  133.9 1.9 %collective-permute-start.3 = (f32[256,128]{1,0:T(8,128)S(1)}, f32[256,128]{1,0:T(8,128)S(1)}, u32[]{:S(2)}, u32[]{:S(2)}) collective-permute-start(f32[256,128]{1,0:T(8,128)S(1)} %get-tuple-element.39), channel_id=1, source_target_pairs={{386,0},{258,1},{322,2},{450,3},{390,4},{262,5},{326,6},{454,7},{3... | collective-permute-start | bytes 393224 | tf_op jit(solution)/shard_map/ppermute | solution.py:376
  135.8 11.1 %collective-permute-done.3.final = f32[256,128]{1,0:T(8,128)S(1)} collective-permute-done((f32[256,128]{1,0:T(8,128)S(1)}, f32[256,128]{1,0:T(8,128)S(1)}, u32[]{:S(2)}, u32[]{:S(2)}) %collective-permute-start.3) | collective-permute-done | bytes 131104 | tf_op jit(solution)/shard_map/ppermute | solution.py:376
  146.9 1.1 shard_map.126
  (10 shorter events, 0.0 us)
Async XLA Ops:
  0.6 13.5 %copy-start.2 = (f32[2,128,4]{1,2,0:T(4,128)S(1)}, f32[2,128,4]{1,2,0:T(4,128)}, u32[]{:S(2)}) copy-start(f32[2,128,4]{1,2,0:T(4,128)} %param.13) | copy-start | bytes 12292
  0.6 30.8 %copy-start = (f32[2,128,512]{2,1,0:T(8,128)S(1)}, f32[2,128,512]{2,1,0:T(8,128)}, u32[]{:S(2)}) copy-start(f32[2,128,512]{2,1,0:T(8,128)} %win.5) | copy-start | bytes 1572868
  0.7 15.7 %collective-permute-start = (f32[256,128]{1,0:T(8,128)}, f32[256,128]{1,0:T(8,128)S(1)}, u32[]{:S(2)}, u32[]{:S(2)}) collective-permute-start(f32[256,128]{1,0:T(8,128)} %bitcast.30), channel_id=1, source_target_pairs={{0,386},{1,258},{2,322},{3,450},{4,390},{5,262},{6,326},{7,454},{8... | collective-permute-start | bytes 393224 | tf_op jit(solution)/shard_map/ppermute | solution.py:341
  12.2 19.2 %collective-permute-start.1 = (f32[256,128]{1,0:T(8,128)}, f32[256,128]{1,0:T(8,128)S(1)}, u32[]{:S(2)}, u32[]{:S(2)}) collective-permute-start(f32[256,128]{1,0:T(8,128)} %bitcast.31), channel_id=1, source_target_pairs={{0,386},{1,258},{2,322},{3,450},{4,390},{5,262},{6,326},{7,454},{8... | collective-permute-start | bytes 393224 | tf_op jit(solution)/shard_map/ppermute | solution.py:342
  17.5 22.9 %all-to-all-start = ((f32[64,8,128]{2,1,0:T(8,128)}), f32[64,8,128]{2,1,0:T(8,128)S(1)}, u32[]{:S(2)}, u32[]{:S(2)}) async-start(f32[64,8,128]{2,1,0:T(8,128)} %bitcast.4), calls=%async_computation | async-start | bytes 524288 | tf_op jit(solution)/shard_map/all_to_all | solution.py:335
  31.4 9.0 %copy-start.1 = (f32[2,128,128]{2,1,0:T(8,128)S(1)}, f32[2,128,128]{2,1,0:T(8,128)}, u32[]{:S(2)}) copy-start(f32[2,128,128]{2,1,0:T(8,128)} %wout.5) | copy-start | bytes 393220
  110.2 18.0 %collective-permute-start.2 = (f32[344,128]{1,0:T(8,128)S(1)}, f32[344,128]{1,0:T(8,128)S(1)}, u32[]{:S(2)}, u32[]{:S(2)}) collective-permute-start(f32[344,128]{1,0:T(8,128)S(1)} %shard_map.125), channel_id=1, source_target_pairs={{386,0},{258,1},{322,2},{450,3},{390,4},{262,5},{326,6},{454,7},{3... | collective-permute-start | bytes 528392 | tf_op jit(solution)/shard_map/ppermute | solution.py:375
  129.1 17.8 %all-to-all-start.5 = ((f32[16,88,128]{2,1,0:T(8,128)}), f32[16,88,128]{2,1,0:T(8,128)S(1)}, u32[]{:S(2)}, u32[]{:S(2)}) async-start(f32[16,88,128]{2,1,0:T(8,128)} %broadcast_in_dim.10), calls=%async_computation.5 | async-start | bytes 1441792 | tf_op jit(solution)/shard_map/all_to_all | solution.py:335
  133.9 13.1 %collective-permute-start.3 = (f32[256,128]{1,0:T(8,128)S(1)}, f32[256,128]{1,0:T(8,128)S(1)}, u32[]{:S(2)}, u32[]{:S(2)}) collective-permute-start(f32[256,128]{1,0:T(8,128)S(1)} %get-tuple-element.39), channel_id=1, source_target_pairs={{386,0},{258,1},{322,2},{450,3},{390,4},{262,5},{326,6},{454,7},{3... | collective-permute-start | bytes 393224 | tf_op jit(solution)/shard_map/ppermute | solution.py:376

commit v4 on v3

--- a/solution.py
+++ b/solution.py
@@ -39,10 +39,32 @@
     return placed, there, back, fours, planes
 
 
+def halves(a):
+    if isinstance(a, tuple):
+        return a
+    high = a.astype(jnp.bfloat16)
+    return high, (a - high.astype(f32)).astype(jnp.bfloat16)
+
+
+def product(a, b, ca, cb):
+    return lax.dot_general(a, b, (((ca,), (cb,)), ((), ())), preferred_element_type=f32)
+
+
 def dot(a, b, ca, cb):
-    return lax.dot_general(
-        a, b, (((ca,), (cb,)), ((), ())), precision=lax.Precision.HIGH, preferred_element_type=f32
-    )
+    (ah, al), (bh, bl) = halves(a), halves(b)
+    n = bh.shape[1 - cb]
+    if ca == 0:
+        if n > 128:
+            return product(ah, bh, 0, 0) + (product(ah, bl, 0, 0) + product(al, bh, 0, 0))
+        r = product(ah, jnp.concatenate([bh, bl], axis=1), 0, 0)
+        return r[:, :n] + (r[:, n:] + product(al, bh, 0, 0))
+    deep = jnp.concatenate([ah, al], axis=1)
+    if n != 128 or ah.shape[1] != 128:
+        return product(deep, jnp.concatenate([bh, bh], axis=cb), 1, cb) + product(ah, bl, 1, cb)
+    highs = jnp.concatenate([bh, bh], axis=cb)
+    lows = jnp.concatenate([bl, jnp.zeros_like(bl)], axis=cb)
+    r = product(deep, jnp.concatenate([highs, lows], axis=1 - cb), 1, cb)
+    return r[:, :n] + r[:, n:]
 
 
 def norm_parts(x):
@@ -61,11 +83,15 @@
 
 
 def by_head(a):
-    lane = lax.broadcasted_iota(jnp.int32, a.shape, 1) // 32
-    return jnp.concatenate([jnp.where(lane == h, a, 0.0) for h in range(4)], axis=0)
+    if isinstance(a, tuple):
+        return tuple(by_head(part) for part in a)
+    lane = lax.broadcasted_iota(jnp.int32, (1, 128), 1) // 32
+    return jnp.concatenate([a * (lane == h).astype(a.dtype) for h in range(4)], axis=0)
 
 
 def side_by_side(a):
+    if isinstance(a, tuple):
+        return tuple(side_by_side(part) for part in a)
     return jnp.concatenate([a[128 * h : 128 * h + 128] for h in range(4)], axis=1)
 
 
@@ -75,36 +101,39 @@
 
 def probabilities(q, k, bias, keys_down):
     if keys_down:
-        e = jnp.exp(dot(by_head(k), q, 1, 1) * SCALE + bias)
-        total = jnp.sum(e.reshape(4, 128, 128), axis=1, keepdims=True)
-        return (e.reshape(4, 128, 128) * (1.0 / total)).reshape(512, 128)
-    e = jnp.exp(dot(by_head(q), k, 1, 1) * SCALE + bias)
+        e = jnp.exp(dot(by_head(halves(k)), q, 1, 1) * SCALE + bias).reshape(4, 128, 128)
+        return (e * (1.0 / jnp.sum(e, axis=1, keepdims=True))).reshape(512, 128)
+    e = jnp.exp(dot(by_head(halves(q)), k, 1, 1) * SCALE + bias)
     return e * (1.0 / jnp.sum(e, axis=1, keepdims=True))
 
 
 def mix(probs, v, keys_down):
     if keys_down:
-        return dot(probs, by_head(v), 0, 0)
-    return dot(side_by_side(probs), by_head(v), 1, 0)
+        return dot(probs, by_head(halves(v)), 0, 0)
+    return dot(side_by_side(halves(probs)), by_head(halves(v)), 1, 0)
 
 
 def attention_back(do, q, k, v, probs, keys_down):
+    do, q, k, v = halves(do), halves(q), halves(k), halves(v)
+    split_probs = halves(probs)
     if keys_down:
         dp = dot(by_head(v), do, 1, 1)
         both_p = (probs * dp).reshape(4, 128, 128)
         ds = (both_p - probs.reshape(4, 128, 128) * jnp.sum(both_p, axis=1, keepdims=True)).reshape(
             512, 128
         )
-        dv = dot(side_by_side(probs), by_head(do), 1, 0)
-        dk = dot(side_by_side(ds), by_head(q), 1, 0) * SCALE
-        dq = dot(ds, by_head(k), 0, 0) * SCALE
+        dv = dot(side_by_side(split_probs), by_head(do), 1, 0)
+        split_ds = halves(ds)
+        dk = dot(side_by_side(split_ds), by_head(q), 1, 0) * SCALE
+        dq = dot(split_ds, by_head(k), 0, 0) * SCALE
     else:
         dp = dot(by_head(do), v, 1, 1)
         both_p = probs * dp
         ds = both_p - probs * jnp.sum(both_p, axis=1, keepdims=True)
-        dv = dot(probs, by_head(do), 0, 0)
-        dk = dot(ds, by_head(q), 0, 0) * SCALE
-        dq = dot(side_by_side(ds), by_head(k), 1, 0) * SCALE
+        dv = dot(split_probs, by_head(do), 0, 0)
+        split_ds = halves(ds)
+        dk = dot(split_ds, by_head(q), 0, 0) * SCALE
+        dq = dot(side_by_side(split_ds), by_head(k), 1, 0) * SCALE
     return ds, dq, dk, dv
 
 
@@ -145,7 +174,7 @@
     for r in range(2):
         part = proj[r * 128 : r * 128 + 128]
         logits_o[r * 512 : r * 512 + 512, :] = (
-            dot(by_head(part[:, 0:128]), part[:, 128:256], 1, 1) * SCALE
+            dot(by_head(halves(part[:, 0:128])), part[:, 128:256], 1, 1) * SCALE
         )
 
 
@@ -297,7 +326,13 @@
     tail[336:344, :] = jnp.sum(shares[...].reshape(4, 32, 128)[:, 20:28, :], axis=0)
 
 
-def last_kernel(recv, tail, final, gin, gbias, gout, grad_o, final_o, rows):
+def emit_kernel(tail, final, grad_o, final_o, mark):
+    grad_o[...] = tail[0:256, :]
+    final_o[...] = final[...]
+    mark[...] = tail[336:344, :]
+
+
+def last_kernel(recv, mark, gin, gbias, gout, rows):
     for j in range(20):
         for k in range(4):
             rows[pl.ds(64 * j + k, 16, stride=4), :] = recv[pl.ds(20 * k + j, 16, stride=88), :]
@@ -309,8 +344,6 @@
     both_bias = jnp.sum(recv[...].reshape(16, 88, 128), axis=0)[80:88]
     gbias[0] = both_bias[0:4]
     gbias[1] = both_bias[4:8]
-    grad_o[...] = tail[0:256, :]
-    final_o[...] = final[...]
 
 
 def call(kernel, outs, *args, cost=None, scratch=()):
@@ -377,10 +410,13 @@
         recv4 = swap(
             jnp.broadcast_to(tail[None, 256:344], (16, 88, 128)).reshape(1408, 128), planes
         )
-        gin, gbias, gout, grad, final = call(
+        grad, final, mark = call(
+            emit_kernel, [(256, 128), (256, 128), (8, 128)], tail, final, cost=LONG
+        )
+        gin, gbias, gout = call(
             last_kernel,
-            [(2, 128, 512), (2, 4, 128), (2, 128, 128), (256, 128), (256, 128)],
-            *(recv4, tail, final),
+            [(2, 128, 512), (2, 4, 128), (2, 128, 128)],
+            *(recv4, mark),
             scratch=[pltpu.VMEM((1280, 128), f32)],
         )
         return (

time: 149 us -> 147 us (0.987)
  the two profiles are of different devices: /device:TPU:66 before, /device:TPU:64 now
where the time goes in v4:
time: 147 us
  blocking collectives  61.3 us (42%)
  starting transfers between devices  36.8 us (25%)
  waiting for transfers between devices  34.9 us (24%)
  Pallas kernels  10.9 us (7%)
  local copies, waits for them, and re-layouts  1.68 us (1%)
    all_to_all x4, blocking collectives, swap(): got = lax.all_to_all(cut, both, 0, 0, axis_index_groups=groups, tiled=True)  61.3 us
    all_to_all x2, waiting for transfers between devices, swap(): got = lax.all_to_all(cut, both, 0, 0, axis_index_groups=groups, tiled=True)  19.5 us
    all_to_all x2, starting transfers between devices, swap(): got = lax.all_to_all(cut, both, 0, 0, axis_index_groups=groups, tiled=True)  17.4 us
    ppermute x1, waiting for transfers between devices, body(): tail = lax.ppermute(tail, both, back)  13.9 us
    ppermute x1, starting transfers between devices, body(): xin = lax.ppermute(pair.reshape(256, 128), both, there)  11.5 us
    pallas_call x9, Pallas kernels, call(): pl.pallas_call(kernel, out_shape=tuple((jax.ShapeDtypeStruct(s, f32) for...  10.9 us
    ppermute x1, starting transfers between devices, body(): tail = lax.ppermute(tail, both, back)  4.1 us
  transfers between devices with their start and end apart: 6, of which 4 were waited for; matrix products, arithmetic and copies ran while one was open for 1% of the time, Pallas kernels for 2%

profile of v4, /device:TPU:64, one launch (start us, length us, event | category | flops | bytes accessed | tf_op | source)
XLA Modules:
  0.0 146.5 jit_solution(13061630548272920133)
XLA Ops:
  0.7 11.5 %collective-permute-start = (f32[256,128]{1,0:T(8,128)}, f32[256,128]{1,0:T(8,128)S(1)}, u32[]{:S(2)}, u32[]{:S(2)}) collective-permute-start(f32[256,128]{1,0:T(8,128)} %bitcast.30), channel_id=1, source_target_pairs={{0,386},{1,258},{2,322},{3,450},{4,390},{5,262},{6,326},{7,454},{8... | collective-permute-start | bytes 393224 | tf_op jit(solution)/shard_map/ppermute | solution.py:374
  12.2 1.9 %collective-permute-start.1 = (f32[256,128]{1,0:T(8,128)}, f32[256,128]{1,0:T(8,128)S(1)}, u32[]{:S(2)}, u32[]{:S(2)}) collective-permute-start(f32[256,128]{1,0:T(8,128)} %bitcast.31), channel_id=1, source_target_pairs={{0,386},{1,258},{2,322},{3,450},{4,390},{5,262},{6,326},{7,454},{8... | collective-permute-start | bytes 393224 | tf_op jit(solution)/shard_map/ppermute | solution.py:375
  14.1 0.7 concatenate.3.small
  14.9 1.5 %collective-permute-done.xin = f32[256,128]{1,0:T(8,128)S(1)} collective-permute-done((f32[256,128]{1,0:T(8,128)}, f32[256,128]{1,0:T(8,128)S(1)}, u32[]{:S(2)}, u32[]{:S(2)}) %collective-permute-start) | collective-permute-done | bytes 131104 | tf_op jit(solution)/shard_map/ppermute | solution.py:374
  16.4 1.1 shard_map.120
  17.5 13.8 %all-to-all-start = ((f32[64,8,128]{2,1,0:T(8,128)}), f32[64,8,128]{2,1,0:T(8,128)S(1)}, u32[]{:S(2)}, u32[]{:S(2)}) async-start(f32[64,8,128]{2,1,0:T(8,128)} %bitcast.4), calls=%async_computation | async-start | bytes 524288 | tf_op jit(solution)/shard_map/all_to_all | solution.py:368
  31.3 0.8 shard_map.119
  32.1 9.1 %all-to-all-done = f32[64,8,128]{2,1,0:T(8,128)S(1)} async-done(((f32[64,8,128]{2,1,0:T(8,128)}), f32[64,8,128]{2,1,0:T(8,128)S(1)}, u32[]{:S(2)}, u32[]{:S(2)}) %all-to-all-start) | async-done | bytes 262176 | tf_op jit(solution)/shard_map/all_to_all | solution.py:368
  41.2 0.9 shard_map.121
  42.1 17.0 %all_to_all.30 = f32[64,16,128]{2,1,0:T(8,128)S(1)} all-to-all(f32[64,16,128]{2,1,0:T(8,128)S(1)} %bitcast.25), channel_id=1, replica_groups={{386,258,322,450,390,262,326,454,394,266,330,458,398,270,334,462,402,27..., dimensions={0} | all-to-all | bytes 1048576 | tf_op jit(solution)/shard_map/all_to_all | solution.py:368
  59.1 3.1 %shard_map.122 = (f32[1024,128]{1,0:T(8,128)S(1)}, f32[640,128]{1,0:T(8,128)S(1)}) custom-call(f32[1024,128]{1,0:T(8,128)S(1)} %bitcast.21, f32[16,128]{1,0:T(8,128)S(1)} %concatenate.3.small, f32[2,128,512]{2,1,0:T(8,128)S(1)} %copy-done, f32[2,128,128]{2,1,0:T(8,128)S(1)} %copy-done.1), custom_call_target="tpu_custom_call" | custom-call | tf_op jit(solution)/shard_map/pallas_call | solution.py:350
  62.2 16.9 %all_to_all.31 = f32[64,16,128]{2,1,0:T(8,128)S(1)} all-to-all(f32[64,16,128]{2,1,0:T(8,128)S(1)} %bitcast.26), channel_id=1, replica_groups={{386,258,322,450,390,262,326,454,394,266,330,458,398,270,334,462,402,27..., dimensions={0} | all-to-all | bytes 1048576 | tf_op jit(solution)/shard_map/all_to_all | solution.py:368
  79.1 2.6 %shard_map.123 = (f32[1792,128]{1,0:T(8,128)S(1)}, f32[256,128]{1,0:T(8,128)S(1)}, f32[256,128]{1,0:T(8,128)S(1)}, f32[8,128]{1,0:T(8,128)S(1)}) custom-call(f32[1024,128]{1,0:T(8,128)S(1)} %bitcast.22, f32[256,128]{1,0:T(8,128)S(1)} %get-tuple-element.26.x.xin, f32[256,128]{1,0:T(8,128)S(1)} %get-tuple-element.31.first, ...), custom_call_target="tpu_custom_call" | custom-call | tf_op jit(solution)/shard_map/pallas_call | solution.py:350
  81.7 21.1 %all_to_all.32 = f32[448,4,128]{2,1,0:T(4,128)S(1)} all-to-all(f32[448,4,128]{2,1,0:T(4,128)S(1)} %bitcast.24), channel_id=1, replica_groups={{386,258,322,450,390,262,326,454,394,266,330,458,398,270,334,462,402,27..., dimensions={0} | all-to-all | bytes 1835008 | tf_op jit(solution)/shard_map/all_to_all | solution.py:368
  103.2 6.3 %all_to_all.33 = f32[4,32,128]{2,1,0:T(8,128)S(1)} all-to-all(f32[4,32,128]{2,1,0:T(8,128)S(1)} %bitcast.28), channel_id=1, replica_groups={{386,258,322,450},{390,262,326,454},{394,266,330,458},{398,270,334,462}..., dimensions={0} | all-to-all | bytes 131072 | tf_op jit(solution)/shard_map/all_to_all | solution.py:368
  109.5 0.4 shard_map.125
  109.9 4.1 %collective-permute-start.2 = (f32[344,128]{1,0:T(8,128)S(1)}, f32[344,128]{1,0:T(8,128)S(1)}, u32[]{:S(2)}, u32[]{:S(2)}) collective-permute-start(f32[344,128]{1,0:T(8,128)S(1)} %shard_map.125), channel_id=1, source_target_pairs={{386,0},{258,1},{322,2},{450,3},{390,4},{262,5},{326,6},{454,7},{3... | collective-permute-start | bytes 528392 | tf_op jit(solution)/shard_map/ppermute | solution.py:408
  114.0 1.9 %collective-permute-start.3 = (f32[256,128]{1,0:T(8,128)S(1)}, f32[256,128]{1,0:T(8,128)S(1)}, u32[]{:S(2)}, u32[]{:S(2)}) collective-permute-start(f32[256,128]{1,0:T(8,128)S(1)} %get-tuple-element.40), channel_id=1, source_target_pairs={{386,0},{258,1},{322,2},{450,3},{390,4},{262,5},{326,6},{454,7},{3... | collective-permute-start | bytes 393224 | tf_op jit(solution)/shard_map/ppermute | solution.py:409
  115.9 13.9 %collective-permute-done.2.tail = f32[344,128]{1,0:T(8,128)S(1)} collective-permute-done((f32[344,128]{1,0:T(8,128)S(1)}, f32[344,128]{1,0:T(8,128)S(1)}, u32[]{:S(2)}, u32[]{:S(2)}) %collective-permute-start.2) | collective-permute-done | bytes 176160 | tf_op jit(solution)/shard_map/ppermute | solution.py:408
  129.8 0.9 broadcast_in_dim.10
  130.8 3.6 %all-to-all-start.5 = ((f32[16,88,128]{2,1,0:T(8,128)}), f32[16,88,128]{2,1,0:T(8,128)S(1)}, u32[]{:S(2)}, u32[]{:S(2)}) async-start(f32[16,88,128]{2,1,0:T(8,128)} %broadcast_in_dim.10), calls=%async_computation.5 | async-start | bytes 1441792 | tf_op jit(solution)/shard_map/all_to_all | solution.py:368
  134.4 0.7 shard_map.126
  135.1 10.4 %all-to-all-done.5 = f32[16,88,128]{2,1,0:T(8,128)S(1)} async-done(((f32[16,88,128]{2,1,0:T(8,128)}), f32[16,88,128]{2,1,0:T(8,128)S(1)}, u32[]{:S(2)}, u32[]{:S(2)}) %all-to-all-start.5) | async-done | bytes 720928 | tf_op jit(solution)/shard_map/all_to_all | solution.py:368
  145.5 1.0 shard_map.127
  (11 shorter events, 0.4 us)
Async XLA Ops:
  0.6 13.5 %copy-start.2 = (f32[2,128,4]{1,2,0:T(4,128)S(1)}, f32[2,128,4]{1,2,0:T(4,128)}, u32[]{:S(2)}) copy-start(f32[2,128,4]{1,2,0:T(4,128)} %param.13) | copy-start | bytes 12292
  0.6 30.6 %copy-start = (f32[2,128,512]{2,1,0:T(8,128)S(1)}, f32[2,128,512]{2,1,0:T(8,128)}, u32[]{:S(2)}) copy-start(f32[2,128,512]{2,1,0:T(8,128)} %win.5) | copy-start | bytes 1572868
  0.7 15.7 %collective-permute-start = (f32[256,128]{1,0:T(8,128)}, f32[256,128]{1,0:T(8,128)S(1)}, u32[]{:S(2)}, u32[]{:S(2)}) collective-permute-start(f32[256,128]{1,0:T(8,128)} %bitcast.30), channel_id=1, source_target_pairs={{0,386},{1,258},{2,322},{3,450},{4,390},{5,262},{6,326},{7,454},{8... | collective-permute-start | bytes 393224 | tf_op jit(solution)/shard_map/ppermute | solution.py:374
  12.2 19.1 %collective-permute-start.1 = (f32[256,128]{1,0:T(8,128)}, f32[256,128]{1,0:T(8,128)S(1)}, u32[]{:S(2)}, u32[]{:S(2)}) collective-permute-start(f32[256,128]{1,0:T(8,128)} %bitcast.31), channel_id=1, source_target_pairs={{0,386},{1,258},{2,322},{3,450},{4,390},{5,262},{6,326},{7,454},{8... | collective-permute-start | bytes 393224 | tf_op jit(solution)/shard_map/ppermute | solution.py:375
  17.5 23.7 %all-to-all-start = ((f32[64,8,128]{2,1,0:T(8,128)}), f32[64,8,128]{2,1,0:T(8,128)S(1)}, u32[]{:S(2)}, u32[]{:S(2)}) async-start(f32[64,8,128]{2,1,0:T(8,128)} %bitcast.4), calls=%async_computation | async-start | bytes 524288 | tf_op jit(solution)/shard_map/all_to_all | solution.py:368
  31.3 9.9 %copy-start.1 = (f32[2,128,128]{2,1,0:T(8,128)S(1)}, f32[2,128,128]{2,1,0:T(8,128)}, u32[]{:S(2)}) copy-start(f32[2,128,128]{2,1,0:T(8,128)} %wout.5) | copy-start | bytes 393220
  109.9 19.9 %collective-permute-start.2 = (f32[344,128]{1,0:T(8,128)S(1)}, f32[344,128]{1,0:T(8,128)S(1)}, u32[]{:S(2)}, u32[]{:S(2)}) collective-permute-start(f32[344,128]{1,0:T(8,128)S(1)} %shard_map.125), channel_id=1, source_target_pairs={{386,0},{258,1},{322,2},{450,3},{390,4},{262,5},{326,6},{454,7},{3... | collective-permute-start | bytes 528392 | tf_op jit(solution)/shard_map/ppermute | solution.py:408
  114.0 20.4 %collective-permute-start.3 = (f32[256,128]{1,0:T(8,128)S(1)}, f32[256,128]{1,0:T(8,128)S(1)}, u32[]{:S(2)}, u32[]{:S(2)}) collective-permute-start(f32[256,128]{1,0:T(8,128)S(1)} %get-tuple-element.40), channel_id=1, source_target_pairs={{386,0},{258,1},{322,2},{450,3},{390,4},{262,5},{326,6},{454,7},{3... | collective-permute-start | bytes 393224 | tf_op jit(solution)/shard_map/ppermute | solution.py:409
  130.8 14.7 %all-to-all-start.5 = ((f32[16,88,128]{2,1,0:T(8,128)}), f32[16,88,128]{2,1,0:T(8,128)S(1)}, u32[]{:S(2)}, u32[]{:S(2)}) async-start(f32[16,88,128]{2,1,0:T(8,128)} %broadcast_in_dim.10), calls=%async_computation.5 | async-start | bytes 1441792 | tf_op jit(solution)/shard_map/all_to_all | solution.py:368

commit v5 on v4

--- a/solution.py
+++ b/solution.py
@@ -314,22 +314,28 @@
         shares[32 * k : 32 * k + 32, :] = share
 
 
-def tail_kernel(shares, totals, x, dx_s, small, tail):
+def tail_kernel(shares, totals, x, dx_s, final, small, share, done):
     gain, _, _, wbias = vectors(small)
     unit, root = norm_parts(x[...])
     dy = jnp.concatenate([dot(totals[4 * r : 4 * r + 4, :], wbias[0], 0, 0) for r in range(2)])
     dx = dx_s[...] + norm_back(dy, gain[0:1, :], unit, root)
     for r in range(2):
-        scatter_rows(tail, (r * 128, r * 128 + 1), 2, dx[r * 128 : r * 128 + 128])
+        scatter_rows(done, (r * 128, r * 128 + 1), 2, dx[r * 128 : r * 128 + 128])
+    done[256:512, :] = final[...]
     for k in range(4):
-        tail[256 + 20 * k : 276 + 20 * k, :] = shares[32 * k : 32 * k + 20, :]
-    tail[336:344, :] = jnp.sum(shares[...].reshape(4, 32, 128)[:, 20:28, :], axis=0)
-
-
-def emit_kernel(tail, final, grad_o, final_o, mark):
-    grad_o[...] = tail[0:256, :]
-    final_o[...] = final[...]
-    mark[...] = tail[336:344, :]
+        share[20 * k : 20 * k + 20, :] = shares[32 * k : 32 * k + 20, :]
+    share[80:88, :] = jnp.sum(shares[...].reshape(4, 32, 128)[:, 20:28, :], axis=0)
+
+
+def spread_kernel(share, out):
+    for b in range(16):
+        out[88 * b : 88 * b + 88, :] = share[...]
+
+
+def emit_kernel(done, grad_o, final_o, mark):
+    grad_o[...] = done[0:256, :]
+    final_o[...] = done[256:512, :]
+    mark[...] = done[0:8, :]
 
 
 def last_kernel(recv, mark, gin, gbias, gout, rows):
@@ -400,18 +406,17 @@
         shares, totals = call(
             fourth_kernel, [(128, 128), (8, 128)], recv3, x, gb1, small
         )
-        (tail,) = call(
+        share, done = call(
             tail_kernel,
-            [(344, 128)],
-            *(swap(shares, fours), totals, x, dx, small),
-        )
-        tail = lax.ppermute(tail, both, back)
-        final = lax.ppermute(final, both, back)
-        recv4 = swap(
-            jnp.broadcast_to(tail[None, 256:344], (16, 88, 128)).reshape(1408, 128), planes
-        )
+            [(88, 128), (512, 128)],
+            *(swap(shares, fours), totals, x, dx, final, small),
+        )
+        share = lax.ppermute(share, both, back)
+        done = lax.ppermute(done, both, back)
+        (spread,) = call(spread_kernel, [(1408, 128)], share, cost=LONG)
+        recv4 = swap(spread, planes)
         grad, final, mark = call(
-            emit_kernel, [(256, 128), (256, 128), (8, 128)], tail, final, cost=LONG
+            emit_kernel, [(256, 128), (256, 128), (8, 128)], done, cost=LONG
         )
         gin, gbias, gout = call(
             last_kernel,

time: 147 us -> 143 us (0.973)
  waiting for transfers between devices: 34.9 us -> 30.7 us
    ppermute x2, waiting for transfers between devices: 13.9 us -> 10.5 us  [the longest x1 5.98 us: body(): share = lax.ppermute(share, both, back)]
    pallas_call x9 -> x10, Pallas kernels: 10.9 us -> 11.9 us  [call(): pl.pallas_call(kernel, out_shape=tuple((jax.ShapeDtypeStruct(s, f32) for...]
  transfers between devices with their start and end apart: 6 -> 6, of which waited for: 4 -> 5; matrix products, arithmetic and copies ran while one was open for 1% -> 1% of each run, Pallas kernels for 2% -> 2%
where the time goes in v5:
time: 143 us; the launch traced here: 142 us
  blocking collectives  61.3 us (43%)
  starting transfers between devices  36.8 us (26%)
  waiting for transfers between devices  30.7 us (21%)
  Pallas kernels  11.9 us (8%)
    all_to_all x4, blocking collectives, swap(): got = lax.all_to_all(cut, both, 0, 0, axis_index_groups=groups, tiled=True)  61.3 us
    all_to_all x2, waiting for transfers between devices, swap(): got = lax.all_to_all(cut, both, 0, 0, axis_index_groups=groups, tiled=True)  18.6 us
    all_to_all x2, starting transfers between devices, swap(): got = lax.all_to_all(cut, both, 0, 0, axis_index_groups=groups, tiled=True)  17.4 us
    pallas_call x10, Pallas kernels, call(): pl.pallas_call(kernel, out_shape=tuple((jax.ShapeDtypeStruct(s, f32) for...  11.9 us
    ppermute x1, starting transfers between devices, body(): xin = lax.ppermute(pair.reshape(256, 128), both, there)  11.5 us
    ppermute x1, waiting for transfers between devices, body(): share = lax.ppermute(share, both, back)  5.98 us
    ppermute x1, waiting for transfers between devices, body(): done = lax.ppermute(done, both, back)  4.57 us
    ppermute x1, starting transfers between devices, body(): share = lax.ppermute(share, both, back)  4.1 us
  transfers between devices with their start and end apart: 6, of which 5 were waited for; matrix products, arithmetic and copies ran while one was open for 1% of the time, Pallas kernels for 2%

profile of v5, /device:TPU:64, one launch (start us, length us, event | category | flops | bytes accessed | tf_op | source)
XLA Modules:
  0.0 142.2 jit_solution(10377337432681675169)
XLA Ops:
  0.7 11.5 %collective-permute-start = (f32[256,128]{1,0:T(8,128)}, f32[256,128]{1,0:T(8,128)S(1)}, u32[]{:S(2)}, u32[]{:S(2)}) collective-permute-start(f32[256,128]{1,0:T(8,128)} %bitcast.31), channel_id=1, source_target_pairs={{0,386},{1,258},{2,322},{3,450},{4,390},{5,262},{6,326},{7,454},{8... | collective-permute-start | bytes 393224 | tf_op jit(solution)/shard_map/ppermute | solution.py:380
  12.2 1.9 %collective-permute-start.1 = (f32[256,128]{1,0:T(8,128)}, f32[256,128]{1,0:T(8,128)S(1)}, u32[]{:S(2)}, u32[]{:S(2)}) collective-permute-start(f32[256,128]{1,0:T(8,128)} %bitcast.32), channel_id=1, source_target_pairs={{0,386},{1,258},{2,322},{3,450},{4,390},{5,262},{6,326},{7,454},{8... | collective-permute-start | bytes 393224 | tf_op jit(solution)/shard_map/ppermute | solution.py:381
  14.1 0.7 concatenate.3.small
  14.9 1.5 %collective-permute-done.xin = f32[256,128]{1,0:T(8,128)S(1)} collective-permute-done((f32[256,128]{1,0:T(8,128)}, f32[256,128]{1,0:T(8,128)S(1)}, u32[]{:S(2)}, u32[]{:S(2)}) %collective-permute-start) | collective-permute-done | bytes 131104 | tf_op jit(solution)/shard_map/ppermute | solution.py:380
  16.4 1.1 shard_map.120
  17.5 13.8 %all-to-all-start = ((f32[64,8,128]{2,1,0:T(8,128)}), f32[64,8,128]{2,1,0:T(8,128)S(1)}, u32[]{:S(2)}, u32[]{:S(2)}) async-start(f32[64,8,128]{2,1,0:T(8,128)} %bitcast.4), calls=%async_computation | async-start | bytes 524288 | tf_op jit(solution)/shard_map/all_to_all | solution.py:374
  31.3 0.8 shard_map.119
  32.1 9.1 %all-to-all-done = f32[64,8,128]{2,1,0:T(8,128)S(1)} async-done(((f32[64,8,128]{2,1,0:T(8,128)}), f32[64,8,128]{2,1,0:T(8,128)S(1)}, u32[]{:S(2)}, u32[]{:S(2)}) %all-to-all-start) | async-done | bytes 262176 | tf_op jit(solution)/shard_map/all_to_all | solution.py:374
  41.2 0.9 shard_map.121
  42.1 17.0 %all_to_all.30 = f32[64,16,128]{2,1,0:T(8,128)S(1)} all-to-all(f32[64,16,128]{2,1,0:T(8,128)S(1)} %bitcast.26), channel_id=1, replica_groups={{386,258,322,450,390,262,326,454,394,266,330,458,398,270,334,462,402,27..., dimensions={0} | all-to-all | bytes 1048576 | tf_op jit(solution)/shard_map/all_to_all | solution.py:374
  59.1 3.1 %shard_map.122 = (f32[1024,128]{1,0:T(8,128)S(1)}, f32[640,128]{1,0:T(8,128)S(1)}) custom-call(f32[1024,128]{1,0:T(8,128)S(1)} %bitcast.22, f32[16,128]{1,0:T(8,128)S(1)} %concatenate.3.small, f32[2,128,512]{2,1,0:T(8,128)S(1)} %copy-done, f32[2,128,128]{2,1,0:T(8,128)S(1)} %copy-done.1), custom_call_target="tpu_custom_call" | custom-call | tf_op jit(solution)/shard_map/pallas_call | solution.py:356
  62.2 16.9 %all_to_all.31 = f32[64,16,128]{2,1,0:T(8,128)S(1)} all-to-all(f32[64,16,128]{2,1,0:T(8,128)S(1)} %bitcast.27), channel_id=1, replica_groups={{386,258,322,450,390,262,326,454,394,266,330,458,398,270,334,462,402,27..., dimensions={0} | all-to-all | bytes 1048576 | tf_op jit(solution)/shard_map/all_to_all | solution.py:374
  79.1 2.6 %shard_map.123 = (f32[1792,128]{1,0:T(8,128)S(1)}, f32[256,128]{1,0:T(8,128)S(1)}, f32[256,128]{1,0:T(8,128)S(1)}, f32[8,128]{1,0:T(8,128)S(1)}) custom-call(f32[1024,128]{1,0:T(8,128)S(1)} %bitcast.23, f32[256,128]{1,0:T(8,128)S(1)} %get-tuple-element.28.x.xin, f32[256,128]{1,0:T(8,128)S(1)} %get-tuple-element.33.first, ...), custom_call_target="tpu_custom_call" | custom-call | tf_op jit(solution)/shard_map/pallas_call | solution.py:356
  81.7 21.1 %all_to_all.32 = f32[448,4,128]{2,1,0:T(4,128)S(1)} all-to-all(f32[448,4,128]{2,1,0:T(4,128)S(1)} %bitcast.25), channel_id=1, replica_groups={{386,258,322,450,390,262,326,454,394,266,330,458,398,270,334,462,402,27..., dimensions={0} | all-to-all | bytes 1835008 | tf_op jit(solution)/shard_map/all_to_all | solution.py:374
  103.2 6.3 %all_to_all.33 = f32[4,32,128]{2,1,0:T(8,128)S(1)} all-to-all(f32[4,32,128]{2,1,0:T(8,128)S(1)} %bitcast.29), channel_id=1, replica_groups={{386,258,322,450},{390,262,326,454},{394,266,330,458},{398,270,334,462}..., dimensions={0} | all-to-all | bytes 131072 | tf_op jit(solution)/shard_map/all_to_all | solution.py:374
  109.9 4.1 %collective-permute-start.3 = (f32[88,128]{1,0:T(8,128)S(1)}, f32[88,128]{1,0:T(8,128)S(1)}, u32[]{:S(2)}, u32[]{:S(2)}) collective-permute-start(f32[88,128]{1,0:T(8,128)S(1)} %get-tuple-element.46), channel_id=1, source_target_pairs={{386,0},{258,1},{322,2},{450,3},{390,4},{262,5},{326,6},{454,7},{3... | collective-permute-start | bytes 135176 | tf_op jit(solution)/shard_map/ppermute | solution.py:414
  114.0 1.9 %collective-permute-start.2 = (f32[512,128]{1,0:T(8,128)S(1)}, f32[512,128]{1,0:T(8,128)S(1)}, u32[]{:S(2)}, u32[]{:S(2)}) collective-permute-start(f32[512,128]{1,0:T(8,128)S(1)} %get-tuple-element.43), channel_id=1, source_target_pairs={{386,0},{258,1},{322,2},{450,3},{390,4},{262,5},{326,6},{454,7},{3... | collective-permute-start | bytes 786440 | tf_op jit(solution)/shard_map/ppermute | solution.py:415
  115.9 6.0 %collective-permute-done.3.share = f32[88,128]{1,0:T(8,128)S(1)} collective-permute-done((f32[88,128]{1,0:T(8,128)S(1)}, f32[88,128]{1,0:T(8,128)S(1)}, u32[]{:S(2)}, u32[]{:S(2)}) %collective-permute-start.3) | collective-permute-done | bytes 45088 | tf_op jit(solution)/shard_map/ppermute | solution.py:414
  121.9 0.9 shard_map.127
  122.9 3.6 %all-to-all-start.5 = ((f32[16,88,128]{2,1,0:T(8,128)}), f32[16,88,128]{2,1,0:T(8,128)S(1)}, u32[]{:S(2)}, u32[]{:S(2)}) async-start(f32[16,88,128]{2,1,0:T(8,128)} %bitcast.16), calls=%async_computation.5 | async-start | bytes 1441792 | tf_op jit(solution)/shard_map/all_to_all | solution.py:374
  126.5 4.6 %collective-permute-done.2.done = f32[512,128]{1,0:T(8,128)S(1)} collective-permute-done((f32[512,128]{1,0:T(8,128)S(1)}, f32[512,128]{1,0:T(8,128)S(1)}, u32[]{:S(2)}, u32[]{:S(2)}) %collective-permute-start.2) | collective-permute-done | bytes 262176 | tf_op jit(solution)/shard_map/ppermute | solution.py:415
  131.0 0.7 shard_map.126
  131.7 9.5 %all-to-all-done.5 = f32[16,88,128]{2,1,0:T(8,128)S(1)} async-done(((f32[16,88,128]{2,1,0:T(8,128)}), f32[16,88,128]{2,1,0:T(8,128)S(1)}, u32[]{:S(2)}, u32[]{:S(2)}) %all-to-all-start.5) | async-done | bytes 720928 | tf_op jit(solution)/shard_map/all_to_all | solution.py:374
  141.2 1.0 shard_map.128
  (10 shorter events, 0.7 us)
Async XLA Ops:
  0.6 13.5 %copy-start.2 = (f32[2,128,4]{1,2,0:T(4,128)S(1)}, f32[2,128,4]{1,2,0:T(4,128)}, u32[]{:S(2)}) copy-start(f32[2,128,4]{1,2,0:T(4,128)} %param.13) | copy-start | bytes 12292
  0.6 30.6 %copy-start = (f32[2,128,512]{2,1,0:T(8,128)S(1)}, f32[2,128,512]{2,1,0:T(8,128)}, u32[]{:S(2)}) copy-start(f32[2,128,512]{2,1,0:T(8,128)} %win.5) | copy-start | bytes 1572868
  0.7 15.7 %collective-permute-start = (f32[256,128]{1,0:T(8,128)}, f32[256,128]{1,0:T(8,128)S(1)}, u32[]{:S(2)}, u32[]{:S(2)}) collective-permute-start(f32[256,128]{1,0:T(8,128)} %bitcast.31), channel_id=1, source_target_pairs={{0,386},{1,258},{2,322},{3,450},{4,390},{5,262},{6,326},{7,454},{8... | collective-permute-start | bytes 393224 | tf_op jit(solution)/shard_map/ppermute | solution.py:380
  12.2 19.1 %collective-permute-start.1 = (f32[256,128]{1,0:T(8,128)}, f32[256,128]{1,0:T(8,128)S(1)}, u32[]{:S(2)}, u32[]{:S(2)}) collective-permute-start(f32[256,128]{1,0:T(8,128)} %bitcast.32), channel_id=1, source_target_pairs={{0,386},{1,258},{2,322},{3,450},{4,390},{5,262},{6,326},{7,454},{8... | collective-permute-start | bytes 393224 | tf_op jit(solution)/shard_map/ppermute | solution.py:381
  17.5 23.7 %all-to-all-start = ((f32[64,8,128]{2,1,0:T(8,128)}), f32[64,8,128]{2,1,0:T(8,128)S(1)}, u32[]{:S(2)}, u32[]{:S(2)}) async-start(f32[64,8,128]{2,1,0:T(8,128)} %bitcast.4), calls=%async_computation | async-start | bytes 524288 | tf_op jit(solution)/shard_map/all_to_all | solution.py:374
  31.3 9.9 %copy-start.1 = (f32[2,128,128]{2,1,0:T(8,128)S(1)}, f32[2,128,128]{2,1,0:T(8,128)}, u32[]{:S(2)}) copy-start(f32[2,128,128]{2,1,0:T(8,128)} %wout.5) | copy-start | bytes 393220
  109.9 12.0 %collective-permute-start.3 = (f32[88,128]{1,0:T(8,128)S(1)}, f32[88,128]{1,0:T(8,128)S(1)}, u32[]{:S(2)}, u32[]{:S(2)}) collective-permute-start(f32[88,128]{1,0:T(8,128)S(1)} %get-tuple-element.46), channel_id=1, source_target_pairs={{386,0},{258,1},{322,2},{450,3},{390,4},{262,5},{326,6},{454,7},{3... | collective-permute-start | bytes 135176 | tf_op jit(solution)/shard_map/ppermute | solution.py:414
  114.0 17.0 %collective-permute-start.2 = (f32[512,128]{1,0:T(8,128)S(1)}, f32[512,128]{1,0:T(8,128)S(1)}, u32[]{:S(2)}, u32[]{:S(2)}) collective-permute-start(f32[512,128]{1,0:T(8,128)S(1)} %get-tuple-element.43), channel_id=1, source_target_pairs={{386,0},{258,1},{322,2},{450,3},{390,4},{262,5},{326,6},{454,7},{3... | collective-permute-start | bytes 786440 | tf_op jit(solution)/shard_map/ppermute | solution.py:415
  122.9 18.4 %all-to-all-start.5 = ((f32[16,88,128]{2,1,0:T(8,128)}), f32[16,88,128]{2,1,0:T(8,128)S(1)}, u32[]{:S(2)}, u32[]{:S(2)}) async-start(f32[16,88,128]{2,1,0:T(8,128)} %bitcast.16), calls=%async_computation.5 | async-start | bytes 1441792 | tf_op jit(solution)/shard_map/all_to_all | solution.py:374

commit v6 on v5

--- a/solution.py
+++ b/solution.py
@@ -152,19 +152,42 @@
     return small[0:2, :], small[2:4, :], small[4:6, :], (small[8:12, :], small[12:16, :])
 
 
-def start_kernel(xin, small, out):
-    gain, shift, _, wbias = vectors(small)
+def start_kernel(
+    pair, cot, gain, shift, gate, wb, bias, small, packed, both_v, gain_v, shift_v, gate_v, wb_v, sems
+):
+    copies = [
+        pltpu.make_async_copy(pair, both_v.at[pl.ds(0, 256)], sems.at[0]),
+        pltpu.make_async_copy(gain, gain_v, sems.at[1]),
+        pltpu.make_async_copy(shift, shift_v, sems.at[2]),
+        pltpu.make_async_copy(gate, gate_v, sems.at[3]),
+        pltpu.make_async_copy(wb, wb_v, sems.at[4]),
+        pltpu.make_async_copy(cot, both_v.at[pl.ds(256, 256)], sems.at[5]),
+    ]
+    for copy in copies:
+        copy.start()
+    for copy in copies:
+        copy.wait()
+    packing = pltpu.make_async_copy(both_v, packed, sems.at[6])
+    packing.start()
+    gains, shifts = gain_v[...], shift_v[...]
     rows = []
     for r in range(2):
-        x = gather_rows(xin, (r * 128, r * 128 + 1), 2)
+        x = gather_rows(both_v, (r * 128, r * 128 + 1), 2)
         unit, root = norm_parts(x)
-        rows.append(dot(wbias[0], unit * gain[0:1, :] + shift[0:1, :], 1, 1))
-    block = jnp.concatenate(rows, axis=0)
+        rows.append(dot(wb_v[0], unit * gains[0:1, :] + shifts[0:1, :], 1, 1))
+    bias[...] = jnp.concatenate(rows, axis=0)
+    small[0:8, :] = jnp.concatenate([gains, shifts, gate_v[...], jnp.zeros_like(gains)], axis=0)
+    small[8:16, :] = jnp.concatenate([wb_v[0], wb_v[1]], axis=0)
+    packing.wait()
+
+
+def repeat_kernel(bias, out):
+    block = bias[...]
     for q in range(64):
         out[q * 8 : q * 8 + 8, :] = block
 
 
-def project_kernel(xin, cot, small, win, x_o, proj_o, logits_o):
+def project_kernel(xin, small, win, x_o, proj_o, logits_o):
     gain, shift, _, _ = vectors(small)
     x = jnp.concatenate([gather_rows(xin, (r * 128, r * 128 + 1), 2) for r in range(2)])
     x_o[...] = x
@@ -178,7 +201,7 @@
         )
 
 
-def first_kernel(x, cot, brecv, proj, logits, small, wout, send, probs_o, mixed_o, first_o):
+def first_kernel(x, xin, brecv, proj, logits, small, wout, send, probs_o, mixed_o, first_o):
     gain, shift, gate, wbias = vectors(small)
     bias = jnp.concatenate([gather_rows(brecv, (h, 4 + h), 8) for h in range(4)])
     mixed = []
@@ -201,7 +224,7 @@
         send[q * 16 + 4 : q * 16 + 12, :] = bias_rows
     for r in range(2):
         scatter_rows(send, (r * 2, r * 2 + 1), 16, first[r * 128 : r * 128 + 128])
-        rows = gather_rows(cot, (r * 128, r * 128 + 1), 2)
+        rows = gather_rows(xin, (256 + r * 128, 256 + r * 128 + 1), 2)
         scatter_rows(send, (12 + r * 2, 12 + r * 2 + 1), 16, rows)
 
 
@@ -375,22 +398,45 @@
         return got.reshape(a.shape)
 
     def body(pair, cotangent, gain, shift, win, wb, gate, wout):
-        wbias = jnp.transpose(wb, (0, 2, 1)).reshape(8, 128)
-        small = jnp.concatenate([gain, shift, gate, jnp.zeros_like(gate), wbias])
-        xin = lax.ppermute(pair.reshape(256, 128), both, there)
-        cot = lax.ppermute(cotangent.reshape(256, 128), both, there)
-        (bsend,) = call(start_kernel, [(512, 128)], xin, small)
-        brecv = swap(bsend, placed)
+        pair, cotangent = pair.reshape(256, 128), cotangent.reshape(256, 128)
+        wbias = jnp.transpose(wb, (0, 2, 1))
+        bias, small, packed = pl.pallas_call(
+            start_kernel,
+            out_shape=(
+                jax.ShapeDtypeStruct((8, 128), f32),
+                jax.ShapeDtypeStruct((16, 128), f32),
+                jax.ShapeDtypeStruct((512, 128), f32),
+            ),
+            in_specs=[pl.BlockSpec(memory_space=pl.ANY)] * 6,
+            out_specs=(
+                pl.BlockSpec(memory_space=pltpu.VMEM),
+                pl.BlockSpec(memory_space=pltpu.VMEM),
+                pl.BlockSpec(memory_space=pl.ANY),
+            ),
+            scratch_shapes=[
+                pltpu.VMEM((512, 128), f32),
+                pltpu.VMEM((2, 128), f32),
+                pltpu.VMEM((2, 128), f32),
+                pltpu.VMEM((2, 128), f32),
+                pltpu.VMEM((2, 4, 128), f32),
+                pltpu.SemaphoreType.DMA((7,)),
+            ],
+            compiler_params=pltpu.CompilerParams(vmem_limit_bytes=60 * 1024 * 1024),
+        )(pair, cotangent, gain, shift, gate, wbias)
+        bias = lax.ppermute(bias, both, there)
+        xin = lax.ppermute(packed, both, there)
+        (repeated,) = call(repeat_kernel, [(512, 128)], bias, cost=LONG)
+        brecv = swap(repeated, placed)
         x, proj, logits = call(
             project_kernel,
             [(256, 128), (256, 512), (1024, 128)],
-            *(xin, cot, small, win),
+            *(xin, small, win),
             cost=LONG,
         )
         send1, probs, mixed, first = call(
             first_kernel,
             [(1024, 128), (1024, 128), (256, 128), (256, 128)],
-            *(x, cot, brecv, proj, logits, small, wout),
+            *(x, xin, brecv, proj, logits, small, wout),
         )
         recv1 = swap(send1, placed)
         send2, wgrad = call(

time: 143 us -> 139 us (0.972)
  the two profiles are of different devices: /device:TPU:64 before, /device:TPU:32 now
where the time goes in v6:
time: 139 us
  blocking collectives  61.5 us (44%)
  starting transfers between devices  39.6 us (28%)
  waiting for transfers between devices  22.9 us (16%)
  Pallas kernels  13.9 us (10%)
    all_to_all x4, blocking collectives, swap(): got = lax.all_to_all(cut, both, 0, 0, axis_index_groups=groups, tiled=True)  61.5 us
    all_to_all x2, waiting for transfers between devices, swap(): got = lax.all_to_all(cut, both, 0, 0, axis_index_groups=groups, tiled=True)  16.6 us
    all_to_all x2, starting transfers between devices, swap(): got = lax.all_to_all(cut, both, 0, 0, axis_index_groups=groups, tiled=True)  14.8 us
    pallas_call x10, Pallas kernels, call(): pl.pallas_call(kernel, out_shape=tuple((jax.ShapeDtypeStruct(s, f32) for...  11.5 us
    ppermute x1, starting transfers between devices, body(): xin = lax.ppermute(packed, both, there)  11.4 us
    ppermute x1, starting transfers between devices, body(): done = lax.ppermute(done, both, back)  7.61 us
    ppermute x1, waiting for transfers between devices, body(): done = lax.ppermute(done, both, back)  6.26 us
    ppermute x1, starting transfers between devices, body(): bias = lax.ppermute(bias, both, there)  3.83 us
  transfers between devices with their start and end apart: 6, of which 3 were waited for; matrix products, arithmetic and copies ran while one was open for 0% of the time, Pallas kernels for 2%

profile of v6, /device:TPU:32, one launch (start us, length us, event | category | flops | bytes accessed | tf_op | source)
XLA Modules:
  0.0 138.7 jit_solution(2069263365923293303)
XLA Ops:
  0.6 2.4 %shard_map.119 = (f32[8,128]{1,0:T(8,128)}, f32[16,128]{1,0:T(8,128)}, f32[512,128]{1,0:T(8,128)}) custom-call(f32[256,128]{1,0:T(8,128)} %bitcast.28, f32[256,128]{1,0:T(8,128)} %bitcast.29, f32[2,128]{1,0:T(2,128)} %gain.1, f32[2,128]{1,0:T(2,128)} %shift.1, f32[2,128]{1,0:T(2,128)} %gate.1, f32[2,4,128]{2,1,0:T(4,128)} %bitcast.30), custom_call_target="tpu_custom_call" | custom-call | tf_op jit(solution)/shard_map/pallas_call | solution.py:403
  3.0 3.8 %collective-permute-start.1 = (f32[8,128]{1,0:T(8,128)}, f32[8,128]{1,0:T(8,128)S(1)}, u32[]{:S(2)}, u32[]{:S(2)}) collective-permute-start(f32[8,128]{1,0:T(8,128)} %get-tuple-element.34), channel_id=1, source_target_pairs={{0,386},{1,258},{2,322},{3,450},{4,390},{5,262},{6,326},{7,454},{8... | collective-permute-start | bytes 12296 | tf_op jit(solution)/shard_map/ppermute | solution.py:426
  6.9 11.4 %collective-permute-start = (f32[512,128]{1,0:T(8,128)}, f32[512,128]{1,0:T(8,128)S(1)}, u32[]{:S(2)}, u32[]{:S(2)}) collective-permute-start(f32[512,128]{1,0:T(8,128)} %get-tuple-element.31), channel_id=1, source_target_pairs={{0,386},{1,258},{2,322},{3,450},{4,390},{5,262},{6,326},{7,454},{8... | collective-permute-start | bytes 786440 | tf_op jit(solution)/shard_map/ppermute | solution.py:427
  18.3 0.7 shard_map.121
  19.0 11.2 %all-to-all-start = ((f32[64,8,128]{2,1,0:T(8,128)}), f32[64,8,128]{2,1,0:T(8,128)S(1)}, u32[]{:S(2)}, u32[]{:S(2)}) async-start(f32[64,8,128]{2,1,0:T(8,128)} %bitcast.3), calls=%async_computation | async-start | bytes 524288 | tf_op jit(solution)/shard_map/all_to_all | solution.py:397
  30.3 0.8 shard_map.120
  31.1 9.2 %all-to-all-done = f32[64,8,128]{2,1,0:T(8,128)S(1)} async-done(((f32[64,8,128]{2,1,0:T(8,128)}), f32[64,8,128]{2,1,0:T(8,128)S(1)}, u32[]{:S(2)}, u32[]{:S(2)}) %all-to-all-start) | async-done | bytes 262176 | tf_op jit(solution)/shard_map/all_to_all | solution.py:397
  40.2 0.9 shard_map.122
  41.2 16.9 %all_to_all.30 = f32[64,16,128]{2,1,0:T(8,128)S(1)} all-to-all(f32[64,16,128]{2,1,0:T(8,128)S(1)} %bitcast.24), channel_id=1, replica_groups={{386,258,322,450,390,262,326,454,394,266,330,458,398,270,334,462,402,27..., dimensions={0} | all-to-all | bytes 1048576 | tf_op jit(solution)/shard_map/all_to_all | solution.py:397
  58.1 3.1 %shard_map.123 = (f32[1024,128]{1,0:T(8,128)S(1)}, f32[640,128]{1,0:T(8,128)S(1)}) custom-call(f32[1024,128]{1,0:T(8,128)S(1)} %bitcast.20, f32[16,128]{1,0:T(8,128)S(1)} %copy-done.2, f32[2,128,512]{2,1,0:T(8,128)S(1)} %copy-done, f32[2,128,128]{2,1,0:T(8,128)S(1)} %copy-done.1), custom_call_target="tpu_custom_call" | custom-call | tf_op jit(solution)/shard_map/pallas_call | solution.py:379
  61.3 16.9 %all_to_all.31 = f32[64,16,128]{2,1,0:T(8,128)S(1)} all-to-all(f32[64,16,128]{2,1,0:T(8,128)S(1)} %bitcast.25), channel_id=1, replica_groups={{386,258,322,450,390,262,326,454,394,266,330,458,398,270,334,462,402,27..., dimensions={0} | all-to-all | bytes 1048576 | tf_op jit(solution)/shard_map/all_to_all | solution.py:397
  78.2 2.6 %shard_map.124 = (f32[1792,128]{1,0:T(8,128)S(1)}, f32[256,128]{1,0:T(8,128)S(1)}, f32[256,128]{1,0:T(8,128)S(1)}, f32[8,128]{1,0:T(8,128)S(1)}) custom-call(f32[1024,128]{1,0:T(8,128)S(1)} %bitcast.21, f32[256,128]{1,0:T(8,128)S(1)} %get-tuple-element.33.x.xin, f32[256,128]{1,0:T(8,128)S(1)} %get-tuple-element.39.first, ...), custom_call_target="tpu_custom_call" | custom-call | tf_op jit(solution)/shard_map/pallas_call | solution.py:379
  80.8 21.1 %all_to_all.32 = f32[448,4,128]{2,1,0:T(4,128)S(1)} all-to-all(f32[448,4,128]{2,1,0:T(4,128)S(1)} %bitcast.23), channel_id=1, replica_groups={{386,258,322,450,390,262,326,454,394,266,330,458,398,270,334,462,402,27..., dimensions={0} | all-to-all | bytes 1835008 | tf_op jit(solution)/shard_map/all_to_all | solution.py:397
  101.9 0.3 shard_map.125
  102.2 6.5 %all_to_all.33 = f32[4,32,128]{2,1,0:T(8,128)S(1)} all-to-all(f32[4,32,128]{2,1,0:T(8,128)S(1)} %bitcast.27), channel_id=1, replica_groups={{386,258,322,450},{390,262,326,454},{394,266,330,458},{398,270,334,462}..., dimensions={0} | all-to-all | bytes 131072 | tf_op jit(solution)/shard_map/all_to_all | solution.py:397
  108.7 0.4 shard_map.126
  109.1 2.0 %collective-permute-start.3 = (f32[88,128]{1,0:T(8,128)S(1)}, f32[88,128]{1,0:T(8,128)S(1)}, u32[]{:S(2)}, u32[]{:S(2)}) collective-permute-start(f32[88,128]{1,0:T(8,128)S(1)} %get-tuple-element.52), channel_id=1, source_target_pairs={{386,0},{258,1},{322,2},{450,3},{390,4},{262,5},{326,6},{454,7},{3... | collective-permute-start | bytes 135176 | tf_op jit(solution)/shard_map/ppermute | solution.py:460
  111.1 7.6 %collective-permute-start.2 = (f32[512,128]{1,0:T(8,128)S(1)}, f32[512,128]{1,0:T(8,128)S(1)}, u32[]{:S(2)}, u32[]{:S(2)}) collective-permute-start(f32[512,128]{1,0:T(8,128)S(1)} %get-tuple-element.49), channel_id=1, source_target_pairs={{386,0},{258,1},{322,2},{450,3},{390,4},{262,5},{326,6},{454,7},{3... | collective-permute-start | bytes 786440 | tf_op jit(solution)/shard_map/ppermute | solution.py:461
  118.7 0.9 shard_map.128
  119.6 3.6 %all-to-all-start.5 = ((f32[16,88,128]{2,1,0:T(8,128)}), f32[16,88,128]{2,1,0:T(8,128)S(1)}, u32[]{:S(2)}, u32[]{:S(2)}) async-start(f32[16,88,128]{2,1,0:T(8,128)} %bitcast.15), calls=%async_computation.5 | async-start | bytes 1441792 | tf_op jit(solution)/shard_map/all_to_all | solution.py:397
  123.3 6.3 %collective-permute-done.2.done = f32[512,128]{1,0:T(8,128)S(1)} collective-permute-done((f32[512,128]{1,0:T(8,128)S(1)}, f32[512,128]{1,0:T(8,128)S(1)}, u32[]{:S(2)}, u32[]{:S(2)}) %collective-permute-start.2) | collective-permute-done | bytes 262176 | tf_op jit(solution)/shard_map/ppermute | solution.py:461
  129.5 0.7 shard_map.127
  130.2 7.4 %all-to-all-done.5 = f32[16,88,128]{2,1,0:T(8,128)S(1)} async-done(((f32[16,88,128]{2,1,0:T(8,128)}), f32[16,88,128]{2,1,0:T(8,128)S(1)}, u32[]{:S(2)}, u32[]{:S(2)}) %all-to-all-start.5) | async-done | bytes 720928 | tf_op jit(solution)/shard_map/all_to_all | solution.py:397
  137.7 1.0 shard_map.129
  (9 shorter events, 0.0 us)
Async XLA Ops:
  3.0 15.2 %collective-permute-start.1 = (f32[8,128]{1,0:T(8,128)}, f32[8,128]{1,0:T(8,128)S(1)}, u32[]{:S(2)}, u32[]{:S(2)}) collective-permute-start(f32[8,128]{1,0:T(8,128)} %get-tuple-element.34), channel_id=1, source_target_pairs={{0,386},{1,258},{2,322},{3,450},{4,390},{5,262},{6,326},{7,454},{8... | collective-permute-start | bytes 12296 | tf_op jit(solution)/shard_map/ppermute | solution.py:426
  6.9 23.4 %collective-permute-start = (f32[512,128]{1,0:T(8,128)}, f32[512,128]{1,0:T(8,128)S(1)}, u32[]{:S(2)}, u32[]{:S(2)}) collective-permute-start(f32[512,128]{1,0:T(8,128)} %get-tuple-element.31), channel_id=1, source_target_pairs={{0,386},{1,258},{2,322},{3,450},{4,390},{5,262},{6,326},{7,454},{8... | collective-permute-start | bytes 786440 | tf_op jit(solution)/shard_map/ppermute | solution.py:427
  18.3 12.0 %copy-start.2 = (f32[16,128]{1,0:T(8,128)S(1)}, f32[16,128]{1,0:T(8,128)}, u32[]{:S(2)}) copy-start(f32[16,128]{1,0:T(8,128)} %get-tuple-element.32.small) | copy-start | bytes 24580
  19.0 11.3 %copy-start = (f32[2,128,512]{2,1,0:T(8,128)S(1)}, f32[2,128,512]{2,1,0:T(8,128)}, u32[]{:S(2)}) copy-start(f32[2,128,512]{2,1,0:T(8,128)} %win.5) | copy-start | bytes 1572868
  19.0 21.3 %all-to-all-start = ((f32[64,8,128]{2,1,0:T(8,128)}), f32[64,8,128]{2,1,0:T(8,128)S(1)}, u32[]{:S(2)}, u32[]{:S(2)}) async-start(f32[64,8,128]{2,1,0:T(8,128)} %bitcast.3), calls=%async_computation | async-start | bytes 524288 | tf_op jit(solution)/shard_map/all_to_all | solution.py:397
  30.3 10.0 %copy-start.1 = (f32[2,128,128]{2,1,0:T(8,128)S(1)}, f32[2,128,128]{2,1,0:T(8,128)}, u32[]{:S(2)}) copy-start(f32[2,128,128]{2,1,0:T(8,128)} %wout.5) | copy-start | bytes 393220
  109.1 9.6 %collective-permute-start.3 = (f32[88,128]{1,0:T(8,128)S(1)}, f32[88,128]{1,0:T(8,128)S(1)}, u32[]{:S(2)}, u32[]{:S(2)}) collective-permute-start(f32[88,128]{1,0:T(8,128)S(1)} %get-tuple-element.52), channel_id=1, source_target_pairs={{386,0},{258,1},{322,2},{450,3},{390,4},{262,5},{326,6},{454,7},{3... | collective-permute-start | bytes 135176 | tf_op jit(solution)/shard_map/ppermute | solution.py:460
  111.1 18.4 %collective-permute-start.2 = (f32[512,128]{1,0:T(8,128)S(1)}, f32[512,128]{1,0:T(8,128)S(1)}, u32[]{:S(2)}, u32[]{:S(2)}) collective-permute-start(f32[512,128]{1,0:T(8,128)S(1)} %get-tuple-element.49), channel_id=1, source_target_pairs={{386,0},{258,1},{322,2},{450,3},{390,4},{262,5},{326,6},{454,7},{3... | collective-permute-start | bytes 786440 | tf_op jit(solution)/shard_map/ppermute | solution.py:461
  119.6 18.0 %all-to-all-start.5 = ((f32[16,88,128]{2,1,0:T(8,128)}), f32[16,88,128]{2,1,0:T(8,128)S(1)}, u32[]{:S(2)}, u32[]{:S(2)}) async-start(f32[16,88,128]{2,1,0:T(8,128)} %bitcast.15), calls=%async_computation.5 | async-start | bytes 1441792 | tf_op jit(solution)/shard_map/all_to_all | solution.py:397

commit v7 on v6

--- a/solution.py
+++ b/solution.py
@@ -165,10 +165,17 @@
     ]
     for copy in copies:
         copy.start()
-    for copy in copies:
+    for copy in copies[:5]:
         copy.wait()
-    packing = pltpu.make_async_copy(both_v, packed, sems.at[6])
-    packing.start()
+    packing = [
+        pltpu.make_async_copy(
+            both_v.at[pl.ds(256 * i, 256)], packed.at[pl.ds(256 * i, 256)], sems.at[6 + i]
+        )
+        for i in range(2)
+    ]
+    packing[0].start()
+    copies[5].wait()
+    packing[1].start()
     gains, shifts = gain_v[...], shift_v[...]
     rows = []
     for r in range(2):
@@ -178,7 +185,8 @@
     bias[...] = jnp.concatenate(rows, axis=0)
     small[0:8, :] = jnp.concatenate([gains, shifts, gate_v[...], jnp.zeros_like(gains)], axis=0)
     small[8:16, :] = jnp.concatenate([wb_v[0], wb_v[1]], axis=0)
-    packing.wait()
+    for copy in packing:
+        copy.wait()
 
 
 def repeat_kernel(bias, out):
@@ -419,7 +427,7 @@
                 pltpu.VMEM((2, 128), f32),
                 pltpu.VMEM((2, 128), f32),
                 pltpu.VMEM((2, 4, 128), f32),
-                pltpu.SemaphoreType.DMA((7,)),
+                pltpu.SemaphoreType.DMA((8,)),
             ],
             compiler_params=pltpu.CompilerParams(vmem_limit_bytes=60 * 1024 * 1024),
         )(pair, cotangent, gain, shift, gate, wbias)

time: 139 us -> 139 us (level)
  no operation moved by 1% of the time
where the time goes in v7:
time: 139 us
  blocking collectives  61.5 us (44%)
  starting transfers between devices  39.6 us (28%)
  waiting for transfers between devices  22.9 us (16%)
  Pallas kernels  13.9 us (10%)
    all_to_all x4, blocking collectives, swap(): got = lax.all_to_all(cut, both, 0, 0, axis_index_groups=groups, tiled=True)  61.5 us
    all_to_all x2, waiting for transfers between devices, swap(): got = lax.all_to_all(cut, both, 0, 0, axis_index_groups=groups, tiled=True)  16.6 us
    all_to_all x2, starting transfers between devices, swap(): got = lax.all_to_all(cut, both, 0, 0, axis_index_groups=groups, tiled=True)  14.8 us
    pallas_call x10, Pallas kernels, call(): pl.pallas_call(kernel, out_shape=tuple((jax.ShapeDtypeStruct(s, f32) for...  11.5 us
    ppermute x1, starting transfers between devices, body(): xin = lax.ppermute(packed, both, there)  11.4 us
    ppermute x1, starting transfers between devices, body(): done = lax.ppermute(done, both, back)  7.61 us
    ppermute x1, waiting for transfers between devices, body(): done = lax.ppermute(done, both, back)  6.26 us
    ppermute x1, starting transfers between devices, body(): bias = lax.ppermute(bias, both, there)  3.83 us
  transfers between devices with their start and end apart: 6, of which 3 were waited for; matrix products, arithmetic and copies ran while one was open for 0% of the time, Pallas kernels for 2%

profile of v7, /device:TPU:32, one launch (start us, length us, event | category | flops | bytes accessed | tf_op | source)
XLA Modules:
  0.0 138.7 jit_solution(10727507373400519041)
XLA Ops:
  0.6 2.4 %shard_map.119 = (f32[8,128]{1,0:T(8,128)}, f32[16,128]{1,0:T(8,128)}, f32[512,128]{1,0:T(8,128)}) custom-call(f32[256,128]{1,0:T(8,128)} %bitcast.28, f32[256,128]{1,0:T(8,128)} %bitcast.29, f32[2,128]{1,0:T(2,128)} %gain.1, f32[2,128]{1,0:T(2,128)} %shift.1, f32[2,128]{1,0:T(2,128)} %gate.1, f32[2,4,128]{2,1,0:T(4,128)} %bitcast.30), custom_call_target="tpu_custom_call" | custom-call | tf_op jit(solution)/shard_map/pallas_call | solution.py:411
  3.0 3.8 %collective-permute-start.1 = (f32[8,128]{1,0:T(8,128)}, f32[8,128]{1,0:T(8,128)S(1)}, u32[]{:S(2)}, u32[]{:S(2)}) collective-permute-start(f32[8,128]{1,0:T(8,128)} %get-tuple-element.34), channel_id=1, source_target_pairs={{0,386},{1,258},{2,322},{3,450},{4,390},{5,262},{6,326},{7,454},{8... | collective-permute-start | bytes 12296 | tf_op jit(solution)/shard_map/ppermute | solution.py:434
  6.8 11.4 %collective-permute-start = (f32[512,128]{1,0:T(8,128)}, f32[512,128]{1,0:T(8,128)S(1)}, u32[]{:S(2)}, u32[]{:S(2)}) collective-permute-start(f32[512,128]{1,0:T(8,128)} %get-tuple-element.31), channel_id=1, source_target_pairs={{0,386},{1,258},{2,322},{3,450},{4,390},{5,262},{6,326},{7,454},{8... | collective-permute-start | bytes 786440 | tf_op jit(solution)/shard_map/ppermute | solution.py:435
  18.2 0.7 shard_map.121
  19.0 11.2 %all-to-all-start = ((f32[64,8,128]{2,1,0:T(8,128)}), f32[64,8,128]{2,1,0:T(8,128)S(1)}, u32[]{:S(2)}, u32[]{:S(2)}) async-start(f32[64,8,128]{2,1,0:T(8,128)} %bitcast.3), calls=%async_computation | async-start | bytes 524288 | tf_op jit(solution)/shard_map/all_to_all | solution.py:405
  30.3 0.8 shard_map.120
  31.0 9.2 %all-to-all-done = f32[64,8,128]{2,1,0:T(8,128)S(1)} async-done(((f32[64,8,128]{2,1,0:T(8,128)}), f32[64,8,128]{2,1,0:T(8,128)S(1)}, u32[]{:S(2)}, u32[]{:S(2)}) %all-to-all-start) | async-done | bytes 262176 | tf_op jit(solution)/shard_map/all_to_all | solution.py:405
  40.2 0.9 shard_map.122
  41.2 16.9 %all_to_all.30 = f32[64,16,128]{2,1,0:T(8,128)S(1)} all-to-all(f32[64,16,128]{2,1,0:T(8,128)S(1)} %bitcast.24), channel_id=1, replica_groups={{386,258,322,450,390,262,326,454,394,266,330,458,398,270,334,462,402,27..., dimensions={0} | all-to-all | bytes 1048576 | tf_op jit(solution)/shard_map/all_to_all | solution.py:405
  58.1 3.1 %shard_map.123 = (f32[1024,128]{1,0:T(8,128)S(1)}, f32[640,128]{1,0:T(8,128)S(1)}) custom-call(f32[1024,128]{1,0:T(8,128)S(1)} %bitcast.20, f32[16,128]{1,0:T(8,128)S(1)} %copy-done.2, f32[2,128,512]{2,1,0:T(8,128)S(1)} %copy-done, f32[2,128,128]{2,1,0:T(8,128)S(1)} %copy-done.1), custom_call_target="tpu_custom_call" | custom-call | tf_op jit(solution)/shard_map/pallas_call | solution.py:387
  61.2 16.9 %all_to_all.31 = f32[64,16,128]{2,1,0:T(8,128)S(1)} all-to-all(f32[64,16,128]{2,1,0:T(8,128)S(1)} %bitcast.25), channel_id=1, replica_groups={{386,258,322,450,390,262,326,454,394,266,330,458,398,270,334,462,402,27..., dimensions={0} | all-to-all | bytes 1048576 | tf_op jit(solution)/shard_map/all_to_all | solution.py:405
  78.1 2.6 %shard_map.124 = (f32[1792,128]{1,0:T(8,128)S(1)}, f32[256,128]{1,0:T(8,128)S(1)}, f32[256,128]{1,0:T(8,128)S(1)}, f32[8,128]{1,0:T(8,128)S(1)}) custom-call(f32[1024,128]{1,0:T(8,128)S(1)} %bitcast.21, f32[256,128]{1,0:T(8,128)S(1)} %get-tuple-element.33.x.xin, f32[256,128]{1,0:T(8,128)S(1)} %get-tuple-element.39.first, ...), custom_call_target="tpu_custom_call" | custom-call | tf_op jit(solution)/shard_map/pallas_call | solution.py:387
  80.7 21.1 %all_to_all.32 = f32[448,4,128]{2,1,0:T(4,128)S(1)} all-to-all(f32[448,4,128]{2,1,0:T(4,128)S(1)} %bitcast.23), channel_id=1, replica_groups={{386,258,322,450,390,262,326,454,394,266,330,458,398,270,334,462,402,27..., dimensions={0} | all-to-all | bytes 1835008 | tf_op jit(solution)/shard_map/all_to_all | solution.py:405
  101.9 0.3 shard_map.125
  102.2 6.5 %all_to_all.33 = f32[4,32,128]{2,1,0:T(8,128)S(1)} all-to-all(f32[4,32,128]{2,1,0:T(8,128)S(1)} %bitcast.27), channel_id=1, replica_groups={{386,258,322,450},{390,262,326,454},{394,266,330,458},{398,270,334,462}..., dimensions={0} | all-to-all | bytes 131072 | tf_op jit(solution)/shard_map/all_to_all | solution.py:405
  108.7 0.4 shard_map.126
  109.1 2.0 %collective-permute-start.3 = (f32[88,128]{1,0:T(8,128)S(1)}, f32[88,128]{1,0:T(8,128)S(1)}, u32[]{:S(2)}, u32[]{:S(2)}) collective-permute-start(f32[88,128]{1,0:T(8,128)S(1)} %get-tuple-element.52), channel_id=1, source_target_pairs={{386,0},{258,1},{322,2},{450,3},{390,4},{262,5},{326,6},{454,7},{3... | collective-permute-start | bytes 135176 | tf_op jit(solution)/shard_map/ppermute | solution.py:468
  111.1 7.6 %collective-permute-start.2 = (f32[512,128]{1,0:T(8,128)S(1)}, f32[512,128]{1,0:T(8,128)S(1)}, u32[]{:S(2)}, u32[]{:S(2)}) collective-permute-start(f32[512,128]{1,0:T(8,128)S(1)} %get-tuple-element.49), channel_id=1, source_target_pairs={{386,0},{258,1},{322,2},{450,3},{390,4},{262,5},{326,6},{454,7},{3... | collective-permute-start | bytes 786440 | tf_op jit(solution)/shard_map/ppermute | solution.py:469
  118.7 0.9 shard_map.128
  119.6 3.6 %all-to-all-start.5 = ((f32[16,88,128]{2,1,0:T(8,128)}), f32[16,88,128]{2,1,0:T(8,128)S(1)}, u32[]{:S(2)}, u32[]{:S(2)}) async-start(f32[16,88,128]{2,1,0:T(8,128)} %bitcast.15), calls=%async_computation.5 | async-start | bytes 1441792 | tf_op jit(solution)/shard_map/all_to_all | solution.py:405
  123.2 6.3 %collective-permute-done.2.done = f32[512,128]{1,0:T(8,128)S(1)} collective-permute-done((f32[512,128]{1,0:T(8,128)S(1)}, f32[512,128]{1,0:T(8,128)S(1)}, u32[]{:S(2)}, u32[]{:S(2)}) %collective-permute-start.2) | collective-permute-done | bytes 262176 | tf_op jit(solution)/shard_map/ppermute | solution.py:469
  129.5 0.7 shard_map.127
  130.2 7.4 %all-to-all-done.5 = f32[16,88,128]{2,1,0:T(8,128)S(1)} async-done(((f32[16,88,128]{2,1,0:T(8,128)}), f32[16,88,128]{2,1,0:T(8,128)S(1)}, u32[]{:S(2)}, u32[]{:S(2)}) %all-to-all-start.5) | async-done | bytes 720928 | tf_op jit(solution)/shard_map/all_to_all | solution.py:405
  137.6 1.0 shard_map.129
  (9 shorter events, 0.0 us)
Async XLA Ops:
  3.0 15.2 %collective-permute-start.1 = (f32[8,128]{1,0:T(8,128)}, f32[8,128]{1,0:T(8,128)S(1)}, u32[]{:S(2)}, u32[]{:S(2)}) collective-permute-start(f32[8,128]{1,0:T(8,128)} %get-tuple-element.34), channel_id=1, source_target_pairs={{0,386},{1,258},{2,322},{3,450},{4,390},{5,262},{6,326},{7,454},{8... | collective-permute-start | bytes 12296 | tf_op jit(solution)/shard_map/ppermute | solution.py:434
  6.8 23.4 %collective-permute-start = (f32[512,128]{1,0:T(8,128)}, f32[512,128]{1,0:T(8,128)S(1)}, u32[]{:S(2)}, u32[]{:S(2)}) collective-permute-start(f32[512,128]{1,0:T(8,128)} %get-tuple-element.31), channel_id=1, source_target_pairs={{0,386},{1,258},{2,322},{3,450},{4,390},{5,262},{6,326},{7,454},{8... | collective-permute-start | bytes 786440 | tf_op jit(solution)/shard_map/ppermute | solution.py:435
  18.2 12.0 %copy-start.2 = (f32[16,128]{1,0:T(8,128)S(1)}, f32[16,128]{1,0:T(8,128)}, u32[]{:S(2)}) copy-start(f32[16,128]{1,0:T(8,128)} %get-tuple-element.32.small) | copy-start | bytes 24580
  19.0 11.3 %copy-start = (f32[2,128,512]{2,1,0:T(8,128)S(1)}, f32[2,128,512]{2,1,0:T(8,128)}, u32[]{:S(2)}) copy-start(f32[2,128,512]{2,1,0:T(8,128)} %win.5) | copy-start | bytes 1572868
  19.0 21.3 %all-to-all-start = ((f32[64,8,128]{2,1,0:T(8,128)}), f32[64,8,128]{2,1,0:T(8,128)S(1)}, u32[]{:S(2)}, u32[]{:S(2)}) async-start(f32[64,8,128]{2,1,0:T(8,128)} %bitcast.3), calls=%async_computation | async-start | bytes 524288 | tf_op jit(solution)/shard_map/all_to_all | solution.py:405
  30.2 10.0 %copy-start.1 = (f32[2,128,128]{2,1,0:T(8,128)S(1)}, f32[2,128,128]{2,1,0:T(8,128)}, u32[]{:S(2)}) copy-start(f32[2,128,128]{2,1,0:T(8,128)} %wout.5) | copy-start | bytes 393220
  109.1 9.6 %collective-permute-start.3 = (f32[88,128]{1,0:T(8,128)S(1)}, f32[88,128]{1,0:T(8,128)S(1)}, u32[]{:S(2)}, u32[]{:S(2)}) collective-permute-start(f32[88,128]{1,0:T(8,128)S(1)} %get-tuple-element.52), channel_id=1, source_target_pairs={{386,0},{258,1},{322,2},{450,3},{390,4},{262,5},{326,6},{454,7},{3... | collective-permute-start | bytes 135176 | tf_op jit(solution)/shard_map/ppermute | solution.py:468
  111.1 18.4 %collective-permute-start.2 = (f32[512,128]{1,0:T(8,128)S(1)}, f32[512,128]{1,0:T(8,128)S(1)}, u32[]{:S(2)}, u32[]{:S(2)}) collective-permute-start(f32[512,128]{1,0:T(8,128)S(1)} %get-tuple-element.49), channel_id=1, source_target_pairs={{386,0},{258,1},{322,2},{450,3},{390,4},{262,5},{326,6},{454,7},{3... | collective-permute-start | bytes 786440 | tf_op jit(solution)/shard_map/ppermute | solution.py:469
  119.6 18.0 %all-to-all-start.5 = ((f32[16,88,128]{2,1,0:T(8,128)}), f32[16,88,128]{2,1,0:T(8,128)S(1)}, u32[]{:S(2)}, u32[]{:S(2)}) async-start(f32[16,88,128]{2,1,0:T(8,128)} %bitcast.15), calls=%async_computation.5 | async-start | bytes 1441792 | tf_op jit(solution)/shard_map/all_to_all | solution.py:405

commit v8 on v6

--- a/solution.py
+++ b/solution.py
@@ -383,7 +383,7 @@
         out_specs=tuple(pl.BlockSpec(memory_space=pltpu.VMEM) for _ in outs),
         scratch_shapes=scratch,
         cost_estimate=cost,
-        compiler_params=pltpu.CompilerParams(vmem_limit_bytes=48 * 1024 * 1024),
+        compiler_params=pltpu.CompilerParams(vmem_limit_bytes=28 * 1024 * 1024),
     )(*args)
 
 

time: 139 us -> 139 us (level)
  no operation moved by 1% of the time
where the time goes in v8:
time: 139 us
  blocking collectives  61.5 us (44%)
  starting transfers between devices  39.6 us (28%)
  waiting for transfers between devices  22.9 us (16%)
  Pallas kernels  13.9 us (10%)
    all_to_all x4, blocking collectives, swap(): got = lax.all_to_all(cut, both, 0, 0, axis_index_groups=groups, tiled=True)  61.5 us
    all_to_all x2, waiting for transfers between devices, swap(): got = lax.all_to_all(cut, both, 0, 0, axis_index_groups=groups, tiled=True)  16.6 us
    all_to_all x2, starting transfers between devices, swap(): got = lax.all_to_all(cut, both, 0, 0, axis_index_groups=groups, tiled=True)  14.8 us
    pallas_call x10, Pallas kernels, call(): pl.pallas_call(kernel, out_shape=tuple((jax.ShapeDtypeStruct(s, f32) for...  11.5 us
    ppermute x1, starting transfers between devices, body(): xin = lax.ppermute(packed, both, there)  11.4 us
    ppermute x1, starting transfers between devices, body(): done = lax.ppermute(done, both, back)  7.61 us
    ppermute x1, waiting for transfers between devices, body(): done = lax.ppermute(done, both, back)  6.26 us
    ppermute x1, starting transfers between devices, body(): bias = lax.ppermute(bias, both, there)  3.83 us
  transfers between devices with their start and end apart: 6, of which 3 were waited for; matrix products, arithmetic and copies ran while one was open for 0% of the time, Pallas kernels for 2%

profile of v8, /device:TPU:32, one launch (start us, length us, event | category | flops | bytes accessed | tf_op | source)
XLA Modules:
  0.0 138.7 jit_solution(13799089194033289283)
XLA Ops:
  0.6 2.4 %shard_map.119 = (f32[8,128]{1,0:T(8,128)}, f32[16,128]{1,0:T(8,128)}, f32[512,128]{1,0:T(8,128)}) custom-call(f32[256,128]{1,0:T(8,128)} %bitcast.28, f32[256,128]{1,0:T(8,128)} %bitcast.29, f32[2,128]{1,0:T(2,128)} %gain.1, f32[2,128]{1,0:T(2,128)} %shift.1, f32[2,128]{1,0:T(2,128)} %gate.1, f32[2,4,128]{2,1,0:T(4,128)} %bitcast.30), custom_call_target="tpu_custom_call" | custom-call | tf_op jit(solution)/shard_map/pallas_call | solution.py:403
  3.0 3.8 %collective-permute-start.1 = (f32[8,128]{1,0:T(8,128)}, f32[8,128]{1,0:T(8,128)S(1)}, u32[]{:S(2)}, u32[]{:S(2)}) collective-permute-start(f32[8,128]{1,0:T(8,128)} %get-tuple-element.34), channel_id=1, source_target_pairs={{0,386},{1,258},{2,322},{3,450},{4,390},{5,262},{6,326},{7,454},{8... | collective-permute-start | bytes 12296 | tf_op jit(solution)/shard_map/ppermute | solution.py:426
  6.9 11.4 %collective-permute-start = (f32[512,128]{1,0:T(8,128)}, f32[512,128]{1,0:T(8,128)S(1)}, u32[]{:S(2)}, u32[]{:S(2)}) collective-permute-start(f32[512,128]{1,0:T(8,128)} %get-tuple-element.31), channel_id=1, source_target_pairs={{0,386},{1,258},{2,322},{3,450},{4,390},{5,262},{6,326},{7,454},{8... | collective-permute-start | bytes 786440 | tf_op jit(solution)/shard_map/ppermute | solution.py:427
  18.3 0.7 shard_map.121
  19.0 11.2 %all-to-all-start = ((f32[64,8,128]{2,1,0:T(8,128)}), f32[64,8,128]{2,1,0:T(8,128)S(1)}, u32[]{:S(2)}, u32[]{:S(2)}) async-start(f32[64,8,128]{2,1,0:T(8,128)} %bitcast.3), calls=%async_computation | async-start | bytes 524288 | tf_op jit(solution)/shard_map/all_to_all | solution.py:397
  30.3 0.8 shard_map.120
  31.1 9.2 %all-to-all-done = f32[64,8,128]{2,1,0:T(8,128)S(1)} async-done(((f32[64,8,128]{2,1,0:T(8,128)}), f32[64,8,128]{2,1,0:T(8,128)S(1)}, u32[]{:S(2)}, u32[]{:S(2)}) %all-to-all-start) | async-done | bytes 262176 | tf_op jit(solution)/shard_map/all_to_all | solution.py:397
  40.2 0.9 shard_map.122
  41.2 16.9 %all_to_all.30 = f32[64,16,128]{2,1,0:T(8,128)S(1)} all-to-all(f32[64,16,128]{2,1,0:T(8,128)S(1)} %bitcast.24), channel_id=1, replica_groups={{386,258,322,450,390,262,326,454,394,266,330,458,398,270,334,462,402,27..., dimensions={0} | all-to-all | bytes 1048576 | tf_op jit(solution)/shard_map/all_to_all | solution.py:397
  58.1 3.1 %shard_map.123 = (f32[1024,128]{1,0:T(8,128)S(1)}, f32[640,128]{1,0:T(8,128)S(1)}) custom-call(f32[1024,128]{1,0:T(8,128)S(1)} %bitcast.20, f32[16,128]{1,0:T(8,128)S(1)} %copy-done.2, f32[2,128,512]{2,1,0:T(8,128)S(1)} %copy-done, f32[2,128,128]{2,1,0:T(8,128)S(1)} %copy-done.1), custom_call_target="tpu_custom_call" | custom-call | tf_op jit(solution)/shard_map/pallas_call | solution.py:379
  61.3 16.9 %all_to_all.31 = f32[64,16,128]{2,1,0:T(8,128)S(1)} all-to-all(f32[64,16,128]{2,1,0:T(8,128)S(1)} %bitcast.25), channel_id=1, replica_groups={{386,258,322,450,390,262,326,454,394,266,330,458,398,270,334,462,402,27..., dimensions={0} | all-to-all | bytes 1048576 | tf_op jit(solution)/shard_map/all_to_all | solution.py:397
  78.2 2.6 %shard_map.124 = (f32[1792,128]{1,0:T(8,128)S(1)}, f32[256,128]{1,0:T(8,128)S(1)}, f32[256,128]{1,0:T(8,128)S(1)}, f32[8,128]{1,0:T(8,128)S(1)}) custom-call(f32[1024,128]{1,0:T(8,128)S(1)} %bitcast.21, f32[256,128]{1,0:T(8,128)S(1)} %get-tuple-element.33.x.xin, f32[256,128]{1,0:T(8,128)S(1)} %get-tuple-element.39.first, ...), custom_call_target="tpu_custom_call" | custom-call | tf_op jit(solution)/shard_map/pallas_call | solution.py:379
  80.8 21.1 %all_to_all.32 = f32[448,4,128]{2,1,0:T(4,128)S(1)} all-to-all(f32[448,4,128]{2,1,0:T(4,128)S(1)} %bitcast.23), channel_id=1, replica_groups={{386,258,322,450,390,262,326,454,394,266,330,458,398,270,334,462,402,27..., dimensions={0} | all-to-all | bytes 1835008 | tf_op jit(solution)/shard_map/all_to_all | solution.py:397
  101.9 0.3 shard_map.125
  102.2 6.5 %all_to_all.33 = f32[4,32,128]{2,1,0:T(8,128)S(1)} all-to-all(f32[4,32,128]{2,1,0:T(8,128)S(1)} %bitcast.27), channel_id=1, replica_groups={{386,258,322,450},{390,262,326,454},{394,266,330,458},{398,270,334,462}..., dimensions={0} | all-to-all | bytes 131072 | tf_op jit(solution)/shard_map/all_to_all | solution.py:397
  108.7 0.4 shard_map.126
  109.1 2.0 %collective-permute-start.3 = (f32[88,128]{1,0:T(8,128)S(1)}, f32[88,128]{1,0:T(8,128)S(1)}, u32[]{:S(2)}, u32[]{:S(2)}) collective-permute-start(f32[88,128]{1,0:T(8,128)S(1)} %get-tuple-element.52), channel_id=1, source_target_pairs={{386,0},{258,1},{322,2},{450,3},{390,4},{262,5},{326,6},{454,7},{3... | collective-permute-start | bytes 135176 | tf_op jit(solution)/shard_map/ppermute | solution.py:460
  111.1 7.6 %collective-permute-start.2 = (f32[512,128]{1,0:T(8,128)S(1)}, f32[512,128]{1,0:T(8,128)S(1)}, u32[]{:S(2)}, u32[]{:S(2)}) collective-permute-start(f32[512,128]{1,0:T(8,128)S(1)} %get-tuple-element.49), channel_id=1, source_target_pairs={{386,0},{258,1},{322,2},{450,3},{390,4},{262,5},{326,6},{454,7},{3... | collective-permute-start | bytes 786440 | tf_op jit(solution)/shard_map/ppermute | solution.py:461
  118.7 0.9 shard_map.128
  119.6 3.6 %all-to-all-start.5 = ((f32[16,88,128]{2,1,0:T(8,128)}), f32[16,88,128]{2,1,0:T(8,128)S(1)}, u32[]{:S(2)}, u32[]{:S(2)}) async-start(f32[16,88,128]{2,1,0:T(8,128)} %bitcast.15), calls=%async_computation.5 | async-start | bytes 1441792 | tf_op jit(solution)/shard_map/all_to_all | solution.py:397
  123.3 6.3 %collective-permute-done.2.done = f32[512,128]{1,0:T(8,128)S(1)} collective-permute-done((f32[512,128]{1,0:T(8,128)S(1)}, f32[512,128]{1,0:T(8,128)S(1)}, u32[]{:S(2)}, u32[]{:S(2)}) %collective-permute-start.2) | collective-permute-done | bytes 262176 | tf_op jit(solution)/shard_map/ppermute | solution.py:461
  129.5 0.7 shard_map.127
  130.2 7.4 %all-to-all-done.5 = f32[16,88,128]{2,1,0:T(8,128)S(1)} async-done(((f32[16,88,128]{2,1,0:T(8,128)}), f32[16,88,128]{2,1,0:T(8,128)S(1)}, u32[]{:S(2)}, u32[]{:S(2)}) %all-to-all-start.5) | async-done | bytes 720928 | tf_op jit(solution)/shard_map/all_to_all | solution.py:397
  137.7 1.0 shard_map.129
  (9 shorter events, 0.0 us)
Async XLA Ops:
  3.0 15.2 %collective-permute-start.1 = (f32[8,128]{1,0:T(8,128)}, f32[8,128]{1,0:T(8,128)S(1)}, u32[]{:S(2)}, u32[]{:S(2)}) collective-permute-start(f32[8,128]{1,0:T(8,128)} %get-tuple-element.34), channel_id=1, source_target_pairs={{0,386},{1,258},{2,322},{3,450},{4,390},{5,262},{6,326},{7,454},{8... | collective-permute-start | bytes 12296 | tf_op jit(solution)/shard_map/ppermute | solution.py:426
  6.9 23.4 %collective-permute-start = (f32[512,128]{1,0:T(8,128)}, f32[512,128]{1,0:T(8,128)S(1)}, u32[]{:S(2)}, u32[]{:S(2)}) collective-permute-start(f32[512,128]{1,0:T(8,128)} %get-tuple-element.31), channel_id=1, source_target_pairs={{0,386},{1,258},{2,322},{3,450},{4,390},{5,262},{6,326},{7,454},{8... | collective-permute-start | bytes 786440 | tf_op jit(solution)/shard_map/ppermute | solution.py:427
  18.3 12.0 %copy-start.2 = (f32[16,128]{1,0:T(8,128)S(1)}, f32[16,128]{1,0:T(8,128)}, u32[]{:S(2)}) copy-start(f32[16,128]{1,0:T(8,128)} %get-tuple-element.32.small) | copy-start | bytes 24580
  19.0 11.3 %copy-start = (f32[2,128,512]{2,1,0:T(8,128)S(1)}, f32[2,128,512]{2,1,0:T(8,128)}, u32[]{:S(2)}) copy-start(f32[2,128,512]{2,1,0:T(8,128)} %win.5) | copy-start | bytes 1572868
  19.0 21.3 %all-to-all-start = ((f32[64,8,128]{2,1,0:T(8,128)}), f32[64,8,128]{2,1,0:T(8,128)S(1)}, u32[]{:S(2)}, u32[]{:S(2)}) async-start(f32[64,8,128]{2,1,0:T(8,128)} %bitcast.3), calls=%async_computation | async-start | bytes 524288 | tf_op jit(solution)/shard_map/all_to_all | solution.py:397
  30.3 10.0 %copy-start.1 = (f32[2,128,128]{2,1,0:T(8,128)S(1)}, f32[2,128,128]{2,1,0:T(8,128)}, u32[]{:S(2)}) copy-start(f32[2,128,128]{2,1,0:T(8,128)} %wout.5) | copy-start | bytes 393220
  109.1 9.6 %collective-permute-start.3 = (f32[88,128]{1,0:T(8,128)S(1)}, f32[88,128]{1,0:T(8,128)S(1)}, u32[]{:S(2)}, u32[]{:S(2)}) collective-permute-start(f32[88,128]{1,0:T(8,128)S(1)} %get-tuple-element.52), channel_id=1, source_target_pairs={{386,0},{258,1},{322,2},{450,3},{390,4},{262,5},{326,6},{454,7},{3... | collective-permute-start | bytes 135176 | tf_op jit(solution)/shard_map/ppermute | solution.py:460
  111.1 18.4 %collective-permute-start.2 = (f32[512,128]{1,0:T(8,128)S(1)}, f32[512,128]{1,0:T(8,128)S(1)}, u32[]{:S(2)}, u32[]{:S(2)}) collective-permute-start(f32[512,128]{1,0:T(8,128)S(1)} %get-tuple-element.49), channel_id=1, source_target_pairs={{386,0},{258,1},{322,2},{450,3},{390,4},{262,5},{326,6},{454,7},{3... | collective-permute-start | bytes 786440 | tf_op jit(solution)/shard_map/ppermute | solution.py:461
  119.6 18.0 %all-to-all-start.5 = ((f32[16,88,128]{2,1,0:T(8,128)}), f32[16,88,128]{2,1,0:T(8,128)S(1)}, u32[]{:S(2)}, u32[]{:S(2)}) async-start(f32[16,88,128]{2,1,0:T(8,128)} %bitcast.15), calls=%async_computation.5 | async-start | bytes 1441792 | tf_op jit(solution)/shard_map/all_to_all | solution.py:397
